TPU v7x, 32 devices: a whole 2x2x4 slice. The times are simulated.
32 devices in a mesh: groups: 2 (over y), row: 4 (over z), col: 2 (over x), sub: 2 (over core).
Axes of the slice: x: 2, y: 2, z: 4, core: 2. Of those that a mesh axis runs over, the one named last changes fastest.
Arguments:
- normed: bfloat16 [1536, 8192], P(('groups', 'col', 'sub'), 'row'), parts along dimension 0, may hold values from -6 to 6
- queries: bfloat16 [1536, 8192], P(('groups', 'row'), ('col', 'sub')), parts along dimension 0, may hold values from -6 to 6
- stored_keys: bfloat16 [1536, 1024], P('groups', ('col', 'sub')), parts along dimension 0, may hold values from -6 to 6
- stored_values: bfloat16 [1536, 1024], P('groups', ('col', 'sub')), parts along dimension 0, may hold values from -6 to 6
- upstream: bfloat16 [1536, 8192], P(('groups', 'col', 'sub'), 'row'), parts along dimension 0, may hold values from -6 to 6
- query_weight: bfloat16 [16384, 8192], P(('groups', 'row'), ('col', 'sub')), parts along dimension 0, may hold values from -0.0625 to 0.0625
- key_matrix: bfloat16 [16384, 1024], P(('groups', 'row'), ('col', 'sub')), parts along dimension 0, may hold values from -0.0625 to 0.0625
- value_matrix: bfloat16 [16384, 1024], P(('groups', 'row'), ('col', 'sub')), parts along dimension 0, may hold values from -0.0625 to 0.0625
- output_weight: bfloat16 [16384, 8192], P(('groups', 'col', 'sub'), 'row'), parts along dimension 0, may hold values from -0.0625 to 0.0625
Outputs:
- grad_normed: bfloat16 [1536, 8192], P(('groups', 'col', 'sub'), 'row'), parts along dimension 0
- grad_query: bfloat16 [16384, 8192], P(('groups', 'row'), ('col', 'sub')), parts along dimension 0
- grad_key: bfloat16 [16384, 1024], P(('groups', 'row'), ('col', 'sub')), parts along dimension 0
- grad_value: bfloat16 [16384, 1024], P(('groups', 'row'), ('col', 'sub')), parts along dimension 0
- grad_output: bfloat16 [16384, 8192], P(('groups', 'col', 'sub'), 'row'), parts along dimension 0
There are 2 independent parts, one for each index of `groups`. A program takes and returns all parts, laid end to end along the dimension named above; each array names one. Nothing has to cross between parts.
All inputs are finite; a program needn't handle non-finite values.
Results may differ from a plain program's by a relative error of at most 0.022.
Values may be sent and summed in bfloat16 or wider, within the bound.
No kernel may reach another device: no remote copies, remote signals or barrier semaphores. Data moves between devices by JAX's collectives and lax.ppermute only.
A program may use at most 128 MiB of HBM per device.

v0:
```python
import jax
import jax.numpy as jnp
from jax import lax
from jax.sharding import PartitionSpec as P

QUERY_HEADS = 64
KEY_VALUE_HEADS = 8
HEAD_SIZE = 128
SEQUENCE_LENGTH = 256


def attend(query_token_rows, key_token_rows, value_token_rows, gradient_rows):
    token_count = query_token_rows.shape[0]
    kv_groups = key_token_rows.shape[1] // HEAD_SIZE
    group_width = QUERY_HEADS // KEY_VALUE_HEADS
    score_scale = HEAD_SIZE ** (-0.5)
    query_head_rows = query_token_rows.reshape(token_count, kv_groups, group_width, HEAD_SIZE)
    gradient_heads = gradient_rows.reshape(token_count, kv_groups, group_width, HEAD_SIZE)
    key_head_rows = key_token_rows.reshape(token_count, kv_groups, HEAD_SIZE)
    value_head_rows = value_token_rows.reshape(token_count, kv_groups, HEAD_SIZE)
    scores = (
        jnp.einsum(
            "qagd,kad->agqk", query_head_rows, key_head_rows, preferred_element_type=jnp.float32
        )
        * score_scale
    )
    positions = jnp.arange(token_count, dtype=jnp.int32)
    allowed = positions[None, :] <= positions[:, None]
    scores = jnp.where(allowed, scores, -jnp.inf)
    top_score = jnp.max(scores, axis=-1, keepdims=True)
    raised = jnp.exp(scores - top_score)
    softmax = raised / jnp.sum(raised, axis=-1, keepdims=True)
    soft_bf = softmax.astype(jnp.bfloat16)
    attended = jnp.einsum(
        "agqk,kad->qagd", soft_bf, value_head_rows, preferred_element_type=jnp.float32
    )
    attended = attended.astype(jnp.bfloat16).reshape(token_count, -1)
    soft_grad = jnp.einsum(
        "qagd,kad->agqk", gradient_heads, value_head_rows, preferred_element_type=jnp.float32
    )
    row_dots = jnp.sum(softmax * soft_grad, axis=-1, keepdims=True)
    score_grad = (softmax * (soft_grad - row_dots)).astype(jnp.bfloat16)
    query_grad = (
        jnp.einsum("agqk,kad->qagd", score_grad, key_head_rows, preferred_element_type=jnp.float32)
        * score_scale
    )
    query_grad = query_grad.astype(jnp.bfloat16).reshape(token_count, -1)
    key_gradient = (
        jnp.einsum(
            "agqk,qagd->kad", score_grad, query_head_rows, preferred_element_type=jnp.float32
        )
        * score_scale
    )
    value_gradient = jnp.einsum(
        "agqk,qagd->kad", soft_bf, gradient_heads, preferred_element_type=jnp.float32
    )
    return (
        attended,
        query_grad,
        key_gradient.reshape(token_count, -1),
        value_gradient.reshape(token_count, -1),
    )


def shards(
    normed,
    queries,
    stored_keys,
    stored_values,
    upstream,
    query_weight,
    key_matrix,
    value_matrix,
    output_weight,
):
    tokens = stored_keys.shape[0]
    normed_all, upstream_all = (
        lax.all_gather(normed, ("col", "sub"), axis=0, tiled=True),
        lax.all_gather(upstream, ("col", "sub"), axis=0, tiled=True),
    )
    contract_last = (((1,), (1,)), ((), ()))
    contract_first = (((0,), (0,)), ((), ()))
    partial_sum = lax.dot_general(
        upstream_all, output_weight, contract_last, preferred_element_type=jnp.float32
    )
    attended_gradient = lax.psum(partial_sum.astype(jnp.bfloat16), "row")
    query_token_rows = lax.all_gather(queries, "row", axis=0, tiled=True)
    sequence_list = tokens // SEQUENCE_LENGTH

    def per_sequence(blocks):
        return attend(blocks[0], blocks[1], blocks[2], blocks[3])

    result_list = lax.map(
        per_sequence,
        (
            query_token_rows.reshape(sequence_list, SEQUENCE_LENGTH, -1),
            stored_keys.reshape(sequence_list, SEQUENCE_LENGTH, -1),
            stored_values.reshape(sequence_list, SEQUENCE_LENGTH, -1),
            attended_gradient.reshape(sequence_list, SEQUENCE_LENGTH, -1),
        ),
    )
    attended_all = result_list[0].reshape(tokens, -1)
    query_all = result_list[1].reshape(tokens, -1)
    key_all = result_list[2].reshape(tokens, -1).astype(jnp.bfloat16)
    value_all = result_list[3].reshape(tokens, -1).astype(jnp.bfloat16)
    grad_output = lax.dot_general(
        attended_all, upstream_all, contract_first, preferred_element_type=jnp.float32
    ).astype(jnp.bfloat16)
    grad_query = lax.dot_general(
        normed_all, query_all, contract_first, preferred_element_type=jnp.float32
    ).astype(jnp.bfloat16)
    grad_key = lax.dot_general(
        normed_all, key_all, contract_first, preferred_element_type=jnp.float32
    ).astype(jnp.bfloat16)
    grad_value = lax.dot_general(
        normed_all, value_all, contract_first, preferred_element_type=jnp.float32
    ).astype(jnp.bfloat16)
    summed = lax.dot_general(
        query_all, query_weight, contract_last, preferred_element_type=jnp.float32
    )
    summed = summed + lax.dot_general(
        key_all, key_matrix, contract_last, preferred_element_type=jnp.float32
    )
    grad_normed = lax.psum_scatter(
        (
            summed
            + lax.dot_general(
                value_all, value_matrix, contract_last, preferred_element_type=jnp.float32
            )
        ).astype(jnp.bfloat16),
        ("col", "sub"),
        scatter_dimension=0,
        tiled=True,
    )
    return (grad_normed, grad_query, grad_key, grad_value, grad_output)


def solution(mesh):
    in_specs = (
        P(("groups", "col", "sub"), "row"),
        P(("groups", "row"), ("col", "sub")),
        P("groups", ("col", "sub")),
        P("groups", ("col", "sub")),
        P(("groups", "col", "sub"), "row"),
        P(("groups", "row"), ("col", "sub")),
        P(("groups", "row"), ("col", "sub")),
        P(("groups", "row"), ("col", "sub")),
        P(("groups", "col", "sub"), "row"),
    )
    out_specs = (
        P(("groups", "col", "sub"), "row"),
        P(("groups", "row"), ("col", "sub")),
        P(("groups", "row"), ("col", "sub")),
        P(("groups", "row"), ("col", "sub")),
        P(("groups", "col", "sub"), "row"),
    )
    return jax.shard_map(shards, mesh=mesh, in_specs=in_specs, out_specs=out_specs, check_vma=False)
```

profile of v0, /device:TPU:0, one launch (start us, length us, event | category | flops | bytes accessed | tf_op | source)
XLA Modules:
  0.0 382.2 jit_solution(4376416737587201554)
XLA Ops:
  8.7 32.1 %all-gather.6.cloned.1.call-done = bf16[768,2048]{1,0:T(8,128)(2,1)} async-done(((bf16[192,2048]{1,0:T(8,128)(2,1)}), bf16[768,2048]{1,0:T(8,128)(2,1)}) %all-gather.6.cloned.1.call-update) | async-done | bytes 3145744 | tf_op jit(solution)/shard_map/all_gather | solution.py:79
  40.8 11.9 %convolution_convert_fusion.2 = bf16[768,2048]{1,0:T(8,128)(2,1)} fusion(bf16[768,2048]{1,0:T(8,128)(2,1)} %all-gather.6.cloned.1.call-done, bf16[2048,2048]{1,0:T(8,128)(2,1)} %param.19), kind=kOutput, calls=%fused_computation.35 | convolution fusion | flops 6444023808 | bytes 14680064 | tf_op jit(solution)/shard_map/dot_general | solution.py:83
  52.7 4.6 %copy.50 = bf16[3,256,2048]{1,2,0:T(8,128)(2,1)} copy(bf16[3,256,2048]{2,1,0:T(8,128)(2,1)} %bitcast.157) | data formatting | bytes 6291456 | tf_op jit(solution)/shard_map/reshape | solution.py:99
  58.1 47.9 %all-gather.4.cloned.1.call-done = bf16[768,2048]{1,0:T(8,128)(2,1)} async-done(((bf16[192,2048]{1,0:T(8,128)(2,1)}), bf16[768,2048]{1,0:T(8,128)(2,1)}) %all-gather.4.cloned.1.call-update) | async-done | bytes 3145744 | tf_op jit(solution)/shard_map/all_gather | solution.py:87
  105.9 122.1 %all-reduce.2.cloned.1.call-done = bf16[3,256,2048]{1,2,0:T(8,128)(2,1)} async-done(((bf16[3,256,2048]{1,2,0:T(8,128)(2,1)}), bf16[3,256,2048]{1,2,0:T(8,128)(2,1)}) %all-reduce.2.cloned.1.call-update) | async-done | bytes 3145744 | tf_op jit(solution)/shard_map/psum | solution.py:86
  228.1 90.0 %while.16 = (s32[]{:T(128)}, bf16[3,256,2048]{2,1,0:T(8,128)(2,1)}, bf16[3,256,2048]{2,1,0:T(8,128)(2,1)}, bf16[3,256,256]{2,1,0:T(8,128)(2,1)}, bf16[3,256,256]...) while((s32[]{:T(128)}, bf16[3,256,2048]{2,1,0:T(8,128)(2,1)}, ...), condition=%wide.region_5.6_spmd, body=%wide.region_1.5_spmd.sunk | while | flops 1628107008 | bytes 90162464 | solution.py:93
  231.1 3.5 fusion.78
  237.2 3.1 fusion.79
  242.9 4.0 %fusion.81 = bf16[2,128,256,1]{2,1,3,0:T(8,128)(2,1)} fusion(bf16[256,2,8,128]{0,3,2,1:T(8,128)(2,1)} %bitcast.148, f32[2,8,256,256]{2,3,1,0:T(8,128)} %get-tuple-element.181, f32[2,8,256]{2,1,0:T(8,128)S(1)} %get-tuple-element.182), kind=kOutput, calls=%fused_computation.17.clone.1 | convolution fusion | flops 270532608 | bytes 5390336 | tf_op jit(solution)/shard_map/while/body/eval_jaxpr/agqk,qagd->kad/dot_general | solution.py:54
  250.1 1.5 copy.98
  251.6 3.7 convolution_convert_fusion.6
  255.3 1.5 copy.99
  256.7 1.5 constant_dynamic-update-slice_fusion.6
  261.3 3.5 fusion.78
  267.3 3.1 fusion.79
  272.9 4.0 %fusion.81 = bf16[2,128,256,1]{2,1,3,0:T(8,128)(2,1)} fusion(bf16[256,2,8,128]{0,3,2,1:T(8,128)(2,1)} %bitcast.148, f32[2,8,256,256]{2,3,1,0:T(8,128)} %get-tuple-element.181, f32[2,8,256]{2,1,0:T(8,128)S(1)} %get-tuple-element.182), kind=kOutput, calls=%fused_computation.17.clone.1 | convolution fusion | flops 270532608 | bytes 5390336 | tf_op jit(solution)/shard_map/while/body/eval_jaxpr/agqk,qagd->kad/dot_general | solution.py:54
  280.1 1.5 copy.98
  281.6 3.6 convolution_convert_fusion.6
  291.2 3.5 fusion.78
  297.2 3.1 fusion.79
  302.8 4.0 %fusion.81 = bf16[2,128,256,1]{2,1,3,0:T(8,128)(2,1)} fusion(bf16[256,2,8,128]{0,3,2,1:T(8,128)(2,1)} %bitcast.148, f32[2,8,256,256]{2,3,1,0:T(8,128)} %get-tuple-element.181, f32[2,8,256]{2,1,0:T(8,128)S(1)} %get-tuple-element.182), kind=kOutput, calls=%fused_computation.17.clone.1 | convolution fusion | flops 270532608 | bytes 5390336 | tf_op jit(solution)/shard_map/while/body/eval_jaxpr/agqk,qagd->kad/dot_general | solution.py:54
  310.0 1.5 copy.98
  311.5 3.6 convolution_convert_fusion.6
  315.1 1.5 copy.99
  318.1 2.2 fusion.20
  322.5 6.7 %fusion.19 = f32[768,2048]{1,0:T(8,128)S(1)} fusion(bf16[768,2048]{1,0:T(8,128)(2,1)S(1)} %bitcast.166, bf16[2048,2048]{1,0:T(8,128)(2,1)S(1)} %copy-done.10), kind=kOutput, calls=%fused_computation.41 | convolution fusion | flops 6442450944 | bytes 17825792 | tf_op jit(solution)/shard_map/dot_general | solution.py:118
  329.2 2.8 add_convert_fusion
  332.0 11.4 %convert_bitcast_fusion = bf16[2048,2048]{0,1:T(8,128)(2,1)} fusion(bf16[768,2048]{1,0:T(8,128)(2,1)} %bitcast.165, bf16[768,2048]{1,0:T(8,128)(2,1)} %all-gather.8.cloned.1.call-done), kind=kOutput, calls=%fused_computation.32 | convolution fusion | flops 6446645248 | bytes 14680064 | tf_op jit(solution)/shard_map/dot_general | solution.py:109
  343.4 12.3 %copy.58 = bf16[2048,2048]{1,0:T(8,128)(2,1)} copy(bf16[2048,2048]{0,1:T(8,128)(2,1)} %convert_bitcast_fusion) | data formatting | bytes 16777216
  355.7 2.9 fusion.16
  360.0 2.9 fusion.17
  364.2 11.4 %convolution_convert_fusion.1 = bf16[2048,2048]{1,0:T(8,128)(2,1)} fusion(bf16[768,2048]{1,0:T(8,128)(2,1)} %bitcast.164, bf16[768,2048]{1,0:T(8,128)(2,1)} %all-gather.6.cloned.1.call-done), kind=kOutput, calls=%fused_computation.33 | convolution fusion | flops 6446645248 | bytes 14680064 | tf_op jit(solution)/shard_map/dot_general | solution.py:106
  (111 shorter events, 45.0 us)
Async XLA Ops:
  7.2 310.9 %copy-start = (bf16[2048,256]{1,0:T(8,128)(2,1)S(1)}, bf16[2048,256]{1,0:T(8,128)(2,1)}, u32[]{:S(2)}) copy-start(bf16[2048,256]{1,0:T(8,128)(2,1)} %param.17) | copy-start | bytes 3145732
  7.2 33.7 %all-gather.6.cloned.1.call-start = ((), (), s32[]{:S(2)}) async-start(), calls=%async_computation.2 | async-start | bytes 3932160 | tf_op jit(solution)/shard_map/all_gather | solution.py:79
  7.9 98.0 %all-gather.4.cloned.1.call-start = ((), (), s32[]{:S(2)}) async-start(), calls=%async_computation.1 | async-start | bytes 3932160 | tf_op jit(solution)/shard_map/all_gather | solution.py:87
  8.7 219.4 %all-reduce.2.cloned.1.call-start = ((), (), s32[]{:S(2)}) async-start(), calls=%async_computation.3 | async-start | bytes 6291456 | tf_op jit(solution)/shard_map/psum | solution.py:86
  57.4 274.6 %all-gather.8.cloned.1.call-start = ((), (), s32[]{:S(2)}) async-start(), calls=%async_computation.5 | async-start | bytes 3932160 | tf_op jit(solution)/shard_map/all_gather | solution.py:78
  58.0 317.6 %reduce-scatter.2.cloned.1.call-start = ((), (), s32[]{:S(2)}) async-start(), calls=%async_computation.4 | async-start | bytes 3932160 | tf_op jit(solution)/shard_map/reduce_scatter | solution.py:124
  229.9 4.7 %copy-start.1 = (bf16[1,256,2048]{1,2,0:T(8,128)(2,1)}, bf16[1,256,2048]{1,2,0:T(8,128)(2,1)S(1)}, u32[]{:S(2)}) copy-start(bf16[1,256,2048]{1,2,0:T(8,128)(2,1)S(1)} %copy.96) | copy-start | bytes 3145732 | tf_op jit(solution)/shard_map/while
  236.0 4.3 %copy-start.4 = (bf16[1,256,2048]{1,2,0:T(8,128)(2,1)}, bf16[1,256,2048]{1,2,0:T(8,128)(2,1)S(1)}, u32[]{:S(2)}) copy-start(bf16[1,256,2048]{1,2,0:T(8,128)(2,1)S(1)} %constant_dynamic-slice_fusion.11) | copy-start | bytes 3145732 | tf_op jit(solution)/shard_map/while
  237.2 3.1 copy-start.5
  237.2 3.5 copy-start.3
  240.7 1.2 copy-start.2
  248.6 2.9 copy-start.6
  260.1 4.7 %copy-start.1 = (bf16[1,256,2048]{1,2,0:T(8,128)(2,1)}, bf16[1,256,2048]{1,2,0:T(8,128)(2,1)S(1)}, u32[]{:S(2)}) copy-start(bf16[1,256,2048]{1,2,0:T(8,128)(2,1)S(1)} %copy.96) | copy-start | bytes 3145732 | tf_op jit(solution)/shard_map/while
  266.1 4.3 %copy-start.4 = (bf16[1,256,2048]{1,2,0:T(8,128)(2,1)}, bf16[1,256,2048]{1,2,0:T(8,128)(2,1)S(1)}, u32[]{:S(2)}) copy-start(bf16[1,256,2048]{1,2,0:T(8,128)(2,1)S(1)} %constant_dynamic-slice_fusion.11) | copy-start | bytes 3145732 | tf_op jit(solution)/shard_map/while
  267.3 3.1 copy-start.5
  267.3 3.5 copy-start.3
  270.8 1.2 copy-start.2
  278.7 2.9 copy-start.6
  290.0 4.7 %copy-start.1 = (bf16[1,256,2048]{1,2,0:T(8,128)(2,1)}, bf16[1,256,2048]{1,2,0:T(8,128)(2,1)S(1)}, u32[]{:S(2)}) copy-start(bf16[1,256,2048]{1,2,0:T(8,128)(2,1)S(1)} %copy.96) | copy-start | bytes 3145732 | tf_op jit(solution)/shard_map/while
  296.0 4.3 %copy-start.4 = (bf16[1,256,2048]{1,2,0:T(8,128)(2,1)}, bf16[1,256,2048]{1,2,0:T(8,128)(2,1)S(1)}, u32[]{:S(2)}) copy-start(bf16[1,256,2048]{1,2,0:T(8,128)(2,1)S(1)} %constant_dynamic-slice_fusion.11) | copy-start | bytes 3145732 | tf_op jit(solution)/shard_map/while
  297.2 3.1 copy-start.5
  297.2 3.5 copy-start.3
  300.7 1.2 copy-start.2
  308.5 2.9 copy-start.6
  318.1 3.5 copy-start.10
  318.1 4.4 %copy-start.11 = (bf16[3,256,2048]{2,1,0:T(8,128)(2,1)S(1)}, bf16[3,256,2048]{2,1,0:T(8,128)(2,1)}, u32[]{:S(2)}) copy-start(bf16[3,256,2048]{2,1,0:T(8,128)(2,1)} %get-tuple-element.55) | copy-start | bytes 9437188
  322.5 6.7 %copy-start.8 = (bf16[2048,256]{1,0:T(8,128)(2,1)S(1)}, bf16[2048,256]{1,0:T(8,128)(2,1)}, u32[]{:S(2)}) copy-start(bf16[2048,256]{1,0:T(8,128)(2,1)} %param.18) | copy-start | bytes 3145732
  322.5 6.7 %copy-start.9 = (bf16[3,256,256]{2,1,0:T(8,128)(2,1)S(1)}, bf16[3,256,256]{2,1,0:T(8,128)(2,1)}, u32[]{:S(2)}) copy-start(bf16[3,256,256]{2,1,0:T(8,128)(2,1)} %get-tuple-element.57) | copy-start | bytes 1179652
  343.4 12.3 %copy-start.7 = (bf16[3,256,256]{2,1,0:T(8,128)(2,1)S(1)}, bf16[3,256,256]{2,1,0:T(8,128)(2,1)}, u32[]{:S(2)}) copy-start(bf16[3,256,256]{2,1,0:T(8,128)(2,1)} %get-tuple-element.56) | copy-start | bytes 1179652
Sparse Core Ops, SparseCore 0:
  9.6 31.2 all-gather.5
  42.4 63.4 all-gather.3
  108.3 119.7 all-reduce.1
  229.5 27.5 all-gather.7
  332.1 37.4 reduce-scatter.1
where the time goes:
time: 384 us; the launch traced here: 382 us
  waiting for transfers between devices  204 us (53%)
  matrix products  102 us (27%)
  local copies, waits for them, and re-layouts  59.2 us (15%)
  between operations  13.9 us (4%)
    psum x1, waiting for transfers between devices, shards(): attended_gradient = lax.psum(partial_sum.astype(jnp.bfloat16), 'row')  122 us
    all_gather x1, waiting for transfers between devices, shards(): query_token_rows = lax.all_gather(queries, 'row', axis=0, tiled=True)  47.9 us
    all_gather x1, waiting for transfers between devices, shards(): lax.all_gather(upstream, ('col', 'sub'), axis=0, tiled=True)  32.1 us
    dynamic_update_slice x18, local copies, waits for them, and re-layouts, shards(): lax.map(per_sequence, (query_token_rows.reshape(sequence_list, SEQUENCE_L...  18.8 us
    unnamed x15, local copies, waits for them, and re-layouts  17.2 us
    dynamic_slice x21, local copies, waits for them, and re-layouts, shards(): lax.map(per_sequence, (query_token_rows.reshape(sequence_list, SEQUENCE_L...  16.4 us
    dot_general x3, matrix products, attend(): jnp.einsum('agqk,qagd->kad', soft_bf, gradient_heads, preferred_element_t...  12 us
    dot_general x1, matrix products, shards(): lax.dot_general(upstream_all, output_weight, contract_last, preferred_ele...  11.9 us
  transfers between devices with their start and end apart: 5, of which 3 were waited for; matrix products, arithmetic and copies ran while one was open for 42% of the time, Pallas kernels for 0%

commit v1 on v0

--- a/solution.py
+++ b/solution.py
@@ -1,13 +1,241 @@
+import functools
+
 import jax
 import jax.numpy as jnp
 from jax import lax
+from jax.experimental import pallas as pl
+from jax.experimental.pallas import tpu as pltpu
 from jax.sharding import PartitionSpec as P
 
 QUERY_HEADS = 64
 KEY_VALUE_HEADS = 8
 HEAD_SIZE = 128
 SEQUENCE_LENGTH = 256
-
+SCALE = HEAD_SIZE ** (-0.5)
+LOG2E = 1.4426950408889634
+F32 = jnp.float32
+BF = jnp.bfloat16
+PARAMS = pltpu.CompilerParams(vmem_limit_bytes=24 * 1024 * 1024)
+CONTRACT_LAST = (((1,), (1,)), ((), ()))
+
+def probabilities(keys, head_queries, allowed):
+    scores = lax.dot_general(keys, head_queries, CONTRACT_LAST, preferred_element_type=F32)
+    scores = jnp.where(allowed, scores, -jnp.inf)
+    top = jnp.max(scores, axis=0, keepdims=True)
+    raised = jnp.exp2((scores - top) * (SCALE * LOG2E))
+    total = jnp.sum(raised, axis=0, keepdims=True)
+    return raised * (1.0 / total)
+
+def causal():
+    shape=(SEQUENCE_LENGTH, SEQUENCE_LENGTH)
+    return lax.broadcasted_iota(jnp.int32, shape, 0) <= lax.broadcasted_iota(jnp.int32, shape, 1)
+
+def forward_kernel(heads, q_ref, k_ref, v_ref, o_ref):
+    allowed = causal()
+    keys = k_ref[...]
+    values_t = v_ref[...].T
+    for h in range(heads):
+        cols = slice(h*HEAD_SIZE,(h+1)*HEAD_SIZE)
+        soft = probabilities(keys, q_ref[:, cols], allowed).astype(BF)
+        o_ref[cols, :] = jnp.dot(values_t, soft, preferred_element_type=F32).astype(BF)
+
+def attended_transposed(queries, keys, values):
+    tokens, width = queries.shape
+    kv = keys.shape[1]//HEAD_SIZE
+    gw = width//kv
+    L = SEQUENCE_LENGTH
+    return pl.pallas_call(
+        functools.partial(forward_kernel, gw//HEAD_SIZE),
+        grid=(tokens//L, kv),
+        in_specs=[pl.BlockSpec((L,gw),lambda s,g:(s,g)),
+                  pl.BlockSpec((L,HEAD_SIZE),lambda s,g:(s,g)),
+                  pl.BlockSpec((L,HEAD_SIZE),lambda s,g:(s,g))],
+        out_specs=pl.BlockSpec((gw,L),lambda s,g:(g,s)),
+        out_shape=jax.ShapeDtypeStruct((width,tokens),BF),
+        compiler_params=PARAMS,
+        name="attention_forward",
+        cost_estimate=pl.CostEstimate(flops=4*tokens*L*width, bytes_accessed=4*tokens*width, transcendentals=0),
+    )(queries,keys,values)
+
+def backward_kernel(k, heads, pieces, fresh, place_ref, q_ref, k_ref, v_ref, *rest):
+    piece_refs = rest[:pieces]
+    if fresh:
+        dq_ref, dk_ref, dv_ref, grad_ref = rest[pieces:]
+    else:
+        _, dk_in, dv_in, dq_ref, dk_ref, dv_ref, grad_ref = rest[pieces:]
+    s = pl.program_id(0)
+    L = SEQUENCE_LENGTH
+
+    @pl.when(s == 0)
+    def _():
+        j = 0
+        for ref in piece_refs:
+            rows = ref.shape[0] if ref.shape[0] * 4 == grad_ref.shape[0] else ref.shape[0] // 2
+            for start in range(0, ref.shape[0], rows):
+                offset = pl.multiple_of(place_ref[12 + j], 64)
+                grad_ref[pl.ds(offset, rows), :] = ref[start : start + rows, :]
+                j += 1
+
+    allowed = causal()
+    keys = k_ref[...]
+    values = v_ref[...]
+    keys_t = keys.T
+    row = pl.multiple_of(s * L, L)
+    dk = jnp.zeros((L, HEAD_SIZE), F32)
+    dv = jnp.zeros((L, HEAD_SIZE), F32)
+    for h in range(heads):
+        cols = slice(h * HEAD_SIZE, (h + 1) * HEAD_SIZE)
+        hq = q_ref[:, cols]
+        hg = grad_ref[pl.ds(row, L), cols]
+        soft = probabilities(keys, hq, allowed)
+        soft_grad = lax.dot_general(values, hg, CONTRACT_LAST, preferred_element_type=F32)
+        dots = jnp.sum(soft * soft_grad, axis=0, keepdims=True)
+        score_grad = (soft * (soft_grad - dots)).astype(BF)
+        dv += jnp.dot(soft.astype(BF), hg, preferred_element_type=F32)
+        dk += jnp.dot(score_grad, hq, preferred_element_type=F32) * SCALE
+        dq_t = jnp.dot(keys_t, score_grad, preferred_element_type=F32) * SCALE
+        dq_ref[:, cols] = dq_t.T.astype(BF)
+    if fresh:
+        dk_ref[...] = dk
+        dv_ref[...] = dv
+    else:
+        again = place_ref[8 + k] != 0
+        dk_ref[...] = jnp.where(again, dk_in[...] + dk, dk)
+        dv_ref[...] = jnp.where(again, dv_in[...] + dv, dv)
+
+
+def attention_backward(k, place, queries, keys, values, pieces, earlier):
+    tokens, width = queries.shape
+    quarter = pieces[0].shape[1]
+    L = SEQUENCE_LENGTH
+    small = pl.BlockSpec((L, HEAD_SIZE), lambda s, place: (s, place[4 + k]))
+    wide = pl.BlockSpec((L, quarter), lambda s, place: (s, place[k]))
+    n = len(pieces)
+    fresh = earlier is None
+    spec = pltpu.PrefetchScalarGridSpec(
+        num_scalar_prefetch=1,
+        grid=(tokens // L,),
+        in_specs=[wide, small, small]
+        + [pl.BlockSpec(x.shape, lambda s, place: (0, 0)) for x in pieces]
+        + ([] if fresh else [pl.BlockSpec(memory_space=pl.ANY), small, small]),
+        out_specs=[wide, small, small],
+        scratch_shapes=[pltpu.VMEM((tokens, quarter), BF)],
+    )
+    sums = jax.ShapeDtypeStruct(keys.shape, F32)
+    return pl.pallas_call(
+        functools.partial(backward_kernel, k, quarter // HEAD_SIZE, n, fresh),
+        grid_spec=spec,
+        out_shape=[jax.ShapeDtypeStruct(queries.shape, BF), sums, sums],
+        input_output_aliases={} if fresh else {4 + n: 0, 5 + n: 1, 6 + n: 2},
+        compiler_params=PARAMS,
+        name="attention_backward",
+        cost_estimate=pl.CostEstimate(flops=60 * tokens * L * quarter, bytes_accessed=8 * tokens * quarter, transcendentals=0),
+    )(place, queries, keys, values, *pieces, *([] if fresh else earlier))
+
+
+def partial_kernel(order_ref, first_ref, second_ref, weight_ref, low_ref, high_ref, near_ref, far_ref, own_ref, both_ref):
+    step = pl.program_id(0)
+    rows = first_ref.shape[0]
+
+    @pl.when(step == 0)
+    def _():
+        both_ref[:rows, :] = first_ref[...]
+        both_ref[rows:, :] = second_ref[...]
+
+    product = lax.dot_general(both_ref[...], weight_ref[...], CONTRACT_LAST, preferred_element_type=F32).astype(BF)
+
+    @pl.when(step == 0)
+    def _():
+        low_ref[...] = product[:rows, :]
+        high_ref[...] = product[rows:, :]
+
+    for place, out_ref in ((1, near_ref), (2, far_ref), (3, own_ref)):
+        @pl.when(step == place)
+        def _(out_ref=out_ref):
+            out_ref[...] = product
+
+
+def partial_products(order, first, second, weight):
+    rows, features = first.shape
+    quarter = weight.shape[0] // 4
+    half = jax.ShapeDtypeStruct((rows, quarter), BF)
+    full = jax.ShapeDtypeStruct((2 * rows, quarter), BF)
+    same = lambda shape: pl.BlockSpec(shape, lambda k, order: (0, 0))
+    spec = pltpu.PrefetchScalarGridSpec(
+        num_scalar_prefetch=1,
+        grid=(4,),
+        in_specs=[same(first.shape), same(second.shape), pl.BlockSpec((quarter, features), lambda k, order: (order[k], 0))],
+        out_specs=[same(half.shape)] * 2 + [same(full.shape)] * 3,
+        scratch_shapes=[pltpu.VMEM((2 * rows, features), BF)],
+    )
+    return pl.pallas_call(
+        partial_kernel,
+        grid_spec=spec,
+        out_shape=[half] * 2 + [full] * 3,
+        compiler_params=PARAMS,
+        name="gradient_partial",
+        cost_estimate=pl.CostEstimate(
+            flops=16 * rows * features * quarter,
+            bytes_accessed=2 * (2 * rows * features + 4 * quarter * features + 8 * rows * quarter),
+            transcendentals=0,
+        ),
+    )(order, first, second, weight)
+
+
+def weights_kernel(n_ref, dq_ref, dk_ref, dv_ref, gq_ref, gk_ref, gv_ref):
+    nt = n_ref[...].T
+    gq_ref[...] = jnp.dot(nt, dq_ref[...], preferred_element_type=F32).astype(BF)
+    gk_ref[...] = jnp.dot(nt, dk_ref[...].astype(BF), preferred_element_type=F32).astype(BF)
+    gv_ref[...] = jnp.dot(nt, dv_ref[...].astype(BF), preferred_element_type=F32).astype(BF)
+
+def weight_gradients(normed, dq, dk, dv, block=256):
+    tokens, feats = normed.shape
+    whole = lambda x: pl.BlockSpec(x.shape, lambda i:(0,0))
+    out = lambda x: pl.BlockSpec((block,x.shape[1]), lambda i:(i,0))
+    return pl.pallas_call(
+        weights_kernel, grid=(feats//block,),
+        in_specs=[pl.BlockSpec((tokens,block),lambda i:(0,i)),whole(dq),whole(dk),whole(dv)],
+        out_specs=[out(dq),out(dk),out(dv)],
+        out_shape=[jax.ShapeDtypeStruct((feats,x.shape[1]),BF) for x in (dq,dk,dv)],
+        compiler_params=PARAMS, name="weight_gradients",
+        cost_estimate=pl.CostEstimate(flops=2*tokens*feats*(dq.shape[1]+2*dk.shape[1]), bytes_accessed=2*(tokens*feats*2+feats*(dq.shape[1]+512)), transcendentals=0),
+    )(normed,dq,dk,dv)
+
+def input_kernel(half, place_ref, dq_ref, dk_ref, dv_ref, wq_ref, wk_ref, wv_ref, first_ref, second_ref, total_ref):
+    rows = first_ref.shape[0]
+    here = pl.ds(pl.multiple_of(place_ref[16 + half], 2 * rows), 2 * rows)
+    total = lax.dot_general(dq_ref[here, :], wq_ref[...], CONTRACT_LAST, preferred_element_type=F32)
+    total += lax.dot_general(dk_ref[here, :].astype(BF), wk_ref[...], CONTRACT_LAST, preferred_element_type=F32)
+    total += lax.dot_general(dv_ref[here, :].astype(BF), wv_ref[...], CONTRACT_LAST, preferred_element_type=F32)
+    total_ref[...] = total.astype(BF)
+    first_ref[...] = total_ref[pl.ds(pl.multiple_of(place_ref[18], rows), rows), :]
+    second_ref[...] = total_ref[pl.ds(pl.multiple_of(place_ref[19], rows), rows), :]
+
+
+def input_gradients(half, place, rows, dq, dk, dv, query_weight, key_matrix, value_matrix, block=512):
+    features, width = query_weight.shape
+    small = key_matrix.shape[1]
+    whole = lambda x: pl.BlockSpec(x.shape, lambda i, place: (0, 0))
+    strip = lambda x: pl.BlockSpec((block, x.shape[1]), lambda i, place: (i, 0))
+    spec = pltpu.PrefetchScalarGridSpec(
+        num_scalar_prefetch=1,
+        grid=(features // block,),
+        in_specs=[whole(dq), whole(dk), whole(dv), strip(query_weight), strip(key_matrix), strip(value_matrix)],
+        out_specs=[pl.BlockSpec((rows, block), lambda i, place: (0, i))] * 2,
+        scratch_shapes=[pltpu.VMEM((2 * rows, block), BF)],
+    )
+    return pl.pallas_call(
+        functools.partial(input_kernel, half),
+        grid_spec=spec,
+        out_shape=[jax.ShapeDtypeStruct((rows, features), BF)] * 2,
+        compiler_params=PARAMS,
+        name="input_gradients",
+        cost_estimate=pl.CostEstimate(
+            flops=4 * rows * features * (width + 2 * small),
+            bytes_accessed=2 * ((features + dq.shape[0]) * (width + 2 * small) + 2 * rows * features),
+            transcendentals=0,
+        ),
+    )(place, dq, dk, dv, query_weight, key_matrix, value_matrix)
 
 def attend(query_token_rows, key_token_rows, value_token_rows, gradient_rows):
     token_count = query_token_rows.shape[0]
@@ -62,7 +290,7 @@
     )
 
 
-def shards(
+def general_shards(
     normed,
     queries,
     stored_keys,
@@ -135,6 +363,137 @@
     return (grad_normed, grad_query, grad_key, grad_value, grad_output)
 
 
+def swap(x, axis):
+    return lax.ppermute(x, axis, [(0, 1), (1, 0)])
+
+
+def turn(x, step, n):
+    return lax.ppermute(x, "row", [(i, (i + step) % n) for i in range(n)])
+
+
+def shift(x, step, done, n):
+    pairs = [(i, i + step) for i in range(n) if 0 <= i + step < n and 0 <= i - done * step < n]
+    return lax.ppermute(x, "row", pairs)
+
+
+def after(value, others):
+    return lax.optimization_barrier((value, others))
+
+
+def total(mine, from_left, from_right):
+    return (mine.astype(F32) + from_left.astype(F32) + from_right.astype(F32)).astype(BF)
+
+
+def with_arrived(products, hops):
+    rows = products[0].shape[0]
+    near = jnp.concatenate([products[2][:rows], products[2][rows:] + hops[0]])
+    far = jnp.concatenate([products[3][:rows] + hops[1], products[3][rows:]])
+    return near, far
+
+
+def in_place(parts, here, rows):
+    whole = jnp.zeros((len(parts) * rows, parts[0].shape[1]), parts[0].dtype)
+    for j, part in enumerate(parts):
+        whole = lax.dynamic_update_slice(whole, part, (rows * (here ^ j), 0))
+    return whole
+
+
+def shards(
+    normed,
+    queries,
+    stored_keys,
+    stored_values,
+    upstream,
+    query_weight,
+    key_matrix,
+    value_matrix,
+    output_weight,
+):
+    row = lax.axis_index("row")
+    col = lax.axis_index("col")
+    sub = lax.axis_index("sub")
+    here = 2 * col + sub
+    rows = upstream.shape[0]
+    quarters = [(row + k) % 4 for k in range(4)]
+    order = jnp.stack([quarters[2], quarters[1], quarters[3], quarters[0]]).astype(jnp.int32)
+    visited = [0 * row, 1 - row % 2, 0 * row + 1, row % 2]
+    places = jnp.stack(
+        quarters
+        + [quarter // 2 for quarter in quarters]
+        + visited
+        + [rows * (here ^ j) for j in range(4)]
+        + [2 * rows * (1 - col), 2 * rows * col, rows * (1 - sub), rows * sub]
+    ).astype(jnp.int32)
+
+    normed_all = lax.all_gather(normed, ("col", "sub"), axis=0, tiled=True)
+    ups = [upstream, swap(upstream, "sub"), swap(upstream, "col")]
+    onward_right, onward_left = queries, queries
+    from_lefts, from_rights = [], []
+    for hop in range(3):
+        onward_right = shift(onward_right, 1, hop, 4)
+        onward_left = shift(onward_left, -1, hop, 4)
+        from_lefts.append(onward_right)
+        from_rights.append(onward_left)
+
+    first = partial_products(order, ups[0], ups[1], output_weight)
+    first_hops = turn(first[1], 1, 4), turn(first[0], -1, 4)
+    ups[2], first = after(ups[2], first)
+    ups.append(swap(ups[2], "sub"))
+    second = partial_products(order, ups[2], ups[3], output_weight)
+    second_hops = turn(second[1], 1, 4), turn(second[0], -1, 4)
+    first_hops, second = after(first_hops, second)
+    first_sums = with_arrived(first, first_hops)
+    first_hops = turn(first_sums[0], 1, 4), turn(first_sums[1], -1, 4)
+    second_hops, first_sums = after(second_hops, first_sums)
+    second_sums = with_arrived(second, second_hops)
+    second_hops = turn(second_sums[0], 1, 4), turn(second_sums[1], -1, 4)
+    (from_lefts, from_rights, ups), second_sums = after((from_lefts, from_rights, ups), second_sums)
+    query_all = jnp.zeros((4 * rows, queries.shape[1]), BF)
+    query_all = lax.dynamic_update_slice(query_all, queries, (rows * row, 0))
+    for k in range(1, 4):
+        part = jnp.where(row >= k, from_lefts[k - 1], from_rights[3 - k])
+        query_all = lax.dynamic_update_slice(query_all, part, (rows * quarters[-k], 0))
+    attended = attended_transposed(query_all, stored_keys, stored_values)
+    upstream_all = in_place(ups, here, rows)
+    first_hops, (attended, upstream_all) = after(first_hops, (attended, upstream_all))
+    own = [total(first[4], *first_hops)]
+    left = [turn(own[0], 1, 4)]
+    right = [turn(own[0], -1, 4)]
+    second_hops, own = after(second_hops, own)
+    own.append(total(second[4], *second_hops))
+    left.append(turn(own[1], 1, 4))
+    right.append(turn(own[1], -1, 4))
+
+    def backward(k, pieces, results):
+        return attention_backward(k, places, query_all, stored_keys, stored_values, pieces, results)
+
+    results = backward(0, own, None)
+    (attended, upstream_all), results = after((attended, upstream_all), results)
+    grad_output = jnp.dot(attended, upstream_all, preferred_element_type=F32).astype(BF)
+    (left, right), (results, grad_output) = after((left, right), (results, grad_output))
+    onward = []
+    for a, b in zip(left, right):
+        onward += [a[:rows], b[rows:]]
+    (left, right), onward = after((left, right), onward)
+    opposite = [turn(x, 1 if i % 2 == 0 else -1, 4) for i, x in enumerate(onward)]
+    results = backward(1, right, results)
+    results = backward(3, left, results)
+    opposite, results = after(opposite, results)
+    query_grad, key_grad, value_grad = backward(2, opposite, results)
+
+    weights = (query_grad, key_grad, value_grad, query_weight, key_matrix, value_matrix)
+    to_sub, to_col = input_gradients(0, places, rows, *weights)
+    to_col = to_col + swap(to_sub, "sub")
+    from_col = swap(to_col, "col")
+    weights, to_col = after(weights, to_col)
+    to_sub, kept = input_gradients(1, places, rows, *weights)
+    from_sub = swap(to_sub, "sub")
+    grad_query, grad_key, grad_value = weight_gradients(normed_all, *weights[:3], block=512)
+    (from_col, from_sub), grad_query = after((from_col, from_sub), grad_query)
+    grad_normed = (kept.astype(F32) + from_sub.astype(F32) + from_col.astype(F32)).astype(BF)
+    return (grad_normed, grad_query, grad_key, grad_value, grad_output)
+
+
 def solution(mesh):
     in_specs = (
         P(("groups", "col", "sub"), "row"),
@@ -154,4 +513,5 @@
         P(("groups", "row"), ("col", "sub")),
         P(("groups", "col", "sub"), "row"),
     )
-    return jax.shard_map(shards, mesh=mesh, in_specs=in_specs, out_specs=out_specs, check_vma=False)
+    small = tuple(mesh.shape[axis] for axis in ("row", "col", "sub")) == (4, 2, 2)
+    return jax.shard_map(shards if small else general_shards, mesh=mesh, in_specs=in_specs, out_specs=out_specs, check_vma=False)

time: 384 us -> 241 us (0.63)
  waiting for transfers between devices: 204 us -> 70.6 us
  matrix products: 102 us -> 9.2 us
  Pallas kernels: 0 us -> 75 us
  starting transfers between devices: 0.19 us -> 42.7 us
  local copies, waits for them, and re-layouts: 59.2 us -> 20.3 us
  other arithmetic: 2.76 us -> 7.58 us
    psum x1 -> x0, waiting for transfers between devices: 122 us -> none  [shards(): attended_gradient = lax.psum(partial_sum.astype(jnp.bfloat16), 'row')]
    dot_general x23 -> x1, matrix products: 91.2 us -> 9.2 us  [shards(): jnp.dot(attended, upstream_all, preferred_element_type=F32).astype(BF)]
    all_gather x3 -> x1, waiting for transfers between devices: 80 us -> 0.01 us  [shards(): normed_all = lax.all_gather(normed, ('col', 'sub'), axis=0, tiled=True)]
    pallas_call x0 -> x10, Pallas kernels: none -> 75 us  [the longest x4 25.4 us: attention_backward(): pl.pallas_call(functools.partial(backward_kernel, k, quarter // HEAD_SIZE...]
    ppermute x0 -> x28, waiting for transfers between devices: none -> 70.6 us  [the longest x6 37.2 us: shift(): return lax.ppermute(x, 'row', pairs)]
    ppermute x0 -> x28, starting transfers between devices: none -> 42.7 us  [the longest x16 28.2 us: turn(): return lax.ppermute(x, 'row', [(i, (i + step) % n) for i in range(n)])]
    dynamic_slice x21 -> x0, local copies, waits for them, and re-layouts: 16.4 us -> none  [shards(): lax.map(per_sequence, (query_token_rows.reshape(sequence_list, SEQUENCE_L...]
    dynamic_update_slice x18 -> x5, local copies, waits for them, and re-layouts: 18.8 us -> 3.82 us  [the longest x4 2.56 us: in_place(): whole = lax.dynamic_update_slice(whole, part, (rows * (here ^ j), 0))]
  transfers between devices with their start and end apart: 5 -> 29, of which waited for: 3 -> 10; matrix products, arithmetic and copies ran while one was open for 42% -> 8% of each run, Pallas kernels for 0% -> 31%
where the time goes in v1:
time: 241 us; the launch traced here: 240 us
  Pallas kernels  75 us (31%)
  waiting for transfers between devices  70.6 us (29%)
  starting transfers between devices  42.7 us (18%)
  local copies, waits for them, and re-layouts  20.3 us (8%)
  between operations  14.8 us (6%)
  matrix products  9.2 us (4%)
  other arithmetic  7.58 us (3%)
    ppermute x6, waiting for transfers between devices, shift(): return lax.ppermute(x, 'row', pairs)  37.2 us
    ppermute x16, starting transfers between devices, turn(): return lax.ppermute(x, 'row', [(i, (i + step) % n) for i in range(n)])  28.2 us
    ppermute x16, waiting for transfers between devices, turn(): return lax.ppermute(x, 'row', [(i, (i + step) % n) for i in range(n)])  26.2 us
    pallas_call x4, Pallas kernels, attention_backward(): pl.pallas_call(functools.partial(backward_kernel, k, quarter // HEAD_SIZE...  25.4 us
    pallas_call x1, Pallas kernels, attended_transposed(): pl.pallas_call(functools.partial(forward_kernel, gw // HEAD_SIZE), grid=(...  16.7 us
    unnamed x50, local copies, waits for them, and re-layouts  15.6 us
    pallas_call x2, Pallas kernels, input_gradients(): pl.pallas_call(functools.partial(input_kernel, half), grid_spec=spec, out...  11.4 us
    pallas_call x2, Pallas kernels, partial_products(): pl.pallas_call(partial_kernel, grid_spec=spec, out_shape=[half] * 2 + [fu...  11.2 us
  transfers between devices with their start and end apart: 29, of which 10 were waited for; matrix products, arithmetic and copies ran while one was open for 8% of the time, Pallas kernels for 31%

profile of v1, /device:TPU:0, one launch (start us, length us, event | category | flops | bytes accessed | tf_op | source)
XLA Modules:
  0.0 240.2 jit_solution(924884560484962277)
XLA Ops:
  7.7 2.6 %collective-permute-start.7 = (bf16[192,2048]{1,0:T(8,128)(2,1)}, bf16[192,2048]{1,0:T(8,128)(2,1)}, u32[]{:S(2)}, u32[]{:S(2)}) collective-permute-start(bf16[192,2048]{1,0:T(8,128)(2,1)} %first_ref.1), channel_id=1, source_target_pairs={{0,2},{2,0},{1,3},{3,1},{4,6},{6,4},{5,7},{7,5},{8,10},{10,8},{9,1... | collective-permute-start | bytes 2359304 | tf_op jit(solution)/shard_map/ppermute | solution.py:367
  10.3 4.4 %collective-permute-start = (bf16[192,2048]{1,0:T(8,128)(2,1)}, bf16[192,2048]{1,0:T(8,128)(2,1)}, u32[]{:S(2)}, u32[]{:S(2)}) collective-permute-start(bf16[192,2048]{1,0:T(8,128)(2,1)} %param.10), channel_id=1, source_target_pairs={{0,4},{4,8},{8,12},{1,5},{5,9},{9,13},{2,6},{6,10},{10,14},{3,7},{... | collective-permute-start | bytes 2359304 | tf_op jit(solution)/shard_map/ppermute | solution.py:376
  17.2 3.4 %copy-done.18 = bf16[2048,2048]{1,0:T(8,128)(2,1)S(1)} copy-done((bf16[2048,2048]{1,0:T(8,128)(2,1)S(1)}, bf16[2048,2048]{1,0:T(8,128)(2,1)}, u32[]{:S(2)}) %copy-start.18) | copy-done | bytes 8388632
  20.6 4.9 %gradient_partial.2 = (bf16[192,512]{1,0:T(8,128)(2,1)S(1)}, bf16[192,512]{1,0:T(8,128)(2,1)S(1)}, bf16[384,512]{1,0:T(8,128)(2,1)S(1)}, bf16[384,512]{1,0:T(8,128)(2,1)S(1)}, bf16[384,512]{1,0:T(8,128)(2,1)S(1)}) custom-call(s32[4]{0:T(128)S(1)} %pad_add_fusion.order_ref, bf16[192,2048]{1,0:T(8,128)(2,1)S(1)} %copy-done.8, ...), custom_call_target="tpu_custom_call" | custom-call | flops 3221225472 | bytes 11534336 | tf_op jit(solution)/shard_map/gradient_partial/pallas_call | solution.py:171
  28.8 2.4 %collective-permute-done = bf16[192,2048]{1,0:T(8,128)(2,1)} collective-permute-done((bf16[192,2048]{1,0:T(8,128)(2,1)}, bf16[192,2048]{1,0:T(8,128)(2,1)}, u32[]{:S(2)}, u32[]{:S(2)}) %collective-permute-start) | collective-permute-done | bytes 786464 | tf_op jit(solution)/shard_map/ppermute | solution.py:376
  32.8 3.4 %collective-permute-done.3 = bf16[192,2048]{1,0:T(8,128)(2,1)} collective-permute-done((bf16[192,2048]{1,0:T(8,128)(2,1)}, bf16[192,2048]{1,0:T(8,128)(2,1)}, u32[]{:S(2)}, u32[]{:S(2)}) %collective-permute-start.3) | collective-permute-done | bytes 786464 | tf_op jit(solution)/shard_map/ppermute | solution.py:376
  42.2 3.4 %copy-done.19 = bf16[2048,2048]{1,0:T(8,128)(2,1)S(1)} copy-done((bf16[2048,2048]{1,0:T(8,128)(2,1)S(1)}, bf16[2048,2048]{1,0:T(8,128)(2,1)}, u32[]{:S(2)}) %copy-start.19) | copy-done | bytes 8388632
  45.6 6.3 %gradient_partial.3 = (bf16[192,512]{1,0:T(8,128)(2,1)S(1)}, bf16[192,512]{1,0:T(8,128)(2,1)S(1)}, bf16[384,512]{1,0:T(8,128)(2,1)S(1)}, bf16[384,512]{1,0:T(8,128)(2,1)S(1)}, bf16[384,512]{1,0:T(8,128)(2,1)S(1)}) custom-call(s32[4]{0:T(128)S(1)} %pad_add_fusion.order_ref, bf16[192,2048]{1,0:T(8,128)(2,1)} %collective-permute-done.7.first_ref, ...), custom_call_target="tpu_custom_call" | custom-call | flops 3221225472 | bytes 11534336 | tf_op jit(solution)/shard_map/gradient_partial/pallas_call | solution.py:171
  52.0 2.8 %collective-permute-start.11 = (bf16[192,512]{1,0:T(8,128)(2,1)S(1)}, bf16[192,512]{1,0:T(8,128)(2,1)S(1)}, u32[]{:S(2)}, u32[]{:S(2)}) collective-permute-start(bf16[192,512]{1,0:T(8,128)(2,1)S(1)} %get-tuple-element.106), channel_id=1, source_target_pairs={{0,4},{4,8},{8,12},{12,0},{1,5},{5,9},{9,13},{13,1},{2,6},{6,10},{... | collective-permute-start | bytes 589832 | tf_op jit(solution)/shard_map/ppermute | solution.py:371
  54.8 14.8 %collective-permute-done.10 = bf16[192,512]{1,0:T(8,128)(2,1)S(1)} collective-permute-done((bf16[192,512]{1,0:T(8,128)(2,1)}, bf16[192,512]{1,0:T(8,128)(2,1)S(1)}, u32[]{:S(2)}, u32[]{:S(2)}) %collective-permute-start.10) | collective-permute-done | bytes 196640 | tf_op jit(solution)/shard_map/ppermute | solution.py:371
  69.8 2.3 collective-permute-start.14
  74.2 2.7 %collective-permute-start.13 = (bf16[384,512]{1,0:T(8,128)(2,1)S(1)}, bf16[384,512]{1,0:T(8,128)(2,1)S(1)}, u32[]{:S(2)}, u32[]{:S(2)}) collective-permute-start(bf16[384,512]{1,0:T(8,128)(2,1)S(1)} %pad_maximum_fusion), channel_id=1, source_target_pairs={{0,4},{4,8},{8,12},{12,0},{1,5},{5,9},{9,13},{13,1},{2,6},{6,10},{... | collective-permute-start | bytes 1179656 | tf_op jit(solution)/shard_map/ppermute | solution.py:371
  77.6 2.0 collective-permute-start.17
  79.8 31.4 %collective-permute-done.5 = bf16[192,2048]{1,0:T(8,128)(2,1)S(1)} collective-permute-done((bf16[192,2048]{1,0:T(8,128)(2,1)}, bf16[192,2048]{1,0:T(8,128)(2,1)S(1)}, u32[]{:S(2)}, u32[]{:S(2)}) %collective-permute-start.5) | collective-permute-done | bytes 786464 | tf_op jit(solution)/shard_map/ppermute | solution.py:376
  117.4 16.7 %attention_forward.1 = bf16[2048,768]{1,0:T(8,128)(2,1)S(1)} custom-call(bf16[768,2048]{1,0:T(8,128)(2,1)S(1)} %select_dynamic-update-slice_fusion.q_ref, bf16[768,256]{1,0:T(8,128)(2,1)S(1)} %copy-done.12, bf16[768,256]{1,0:T(8,128)(2,1)S(1)} %copy-done.13), custom_call_target="tpu_custom_call" | custom-call | flops 1610612736 | bytes 6291456 | tf_op jit(solution)/shard_map/attention_forward/pallas_call | solution.py:47
  135.3 3.0 %collective-permute-start.20 = (bf16[384,512]{1,0:T(8,128)(2,1)S(1)}, bf16[384,512]{1,0:T(8,128)(2,1)S(1)}, u32[]{:S(2)}, u32[]{:S(2)}) collective-permute-start(bf16[384,512]{1,0:T(8,128)(2,1)S(1)} %add_convert_fusion.1.rest_1_), channel_id=1, source_target_pairs={{0,12},{4,0},{8,4},{12,8},{1,13},{5,1},{9,5},{13,9},{2,14},{6,2},{... | collective-permute-start | bytes 1179656 | tf_op jit(solution)/shard_map/ppermute | solution.py:371
  138.3 3.8 %collective-permute-start.19 = (bf16[384,512]{1,0:T(8,128)(2,1)S(1)}, bf16[384,512]{1,0:T(8,128)(2,1)S(1)}, u32[]{:S(2)}, u32[]{:S(2)}) collective-permute-start(bf16[384,512]{1,0:T(8,128)(2,1)S(1)} %add_convert_fusion.2.rest_0_), channel_id=1, source_target_pairs={{0,12},{4,0},{8,4},{12,8},{1,13},{5,1},{9,5},{13,9},{2,14},{6,2},{... | collective-permute-start | bytes 1179656 | tf_op jit(solution)/shard_map/ppermute | solution.py:371
  142.1 6.3 %attention_backward.4 = (bf16[768,2048]{1,0:T(8,128)(2,1)S(1)}, f32[768,256]{1,0:T(8,128)S(1)}, f32[768,256]{1,0:T(8,128)S(1)}) custom-call(s32[20]{0:T(128)S(1)} %stack.82.place_ref, bf16[768,2048]{1,0:T(8,128)(2,1)S(1)} %select_dynamic-update-slice_fusion.q_ref, bf16[768,256]{1,0:T(8,128)(2,1)S(1)} %copy-done.12, bf16[768,256]{1,0:T(8,128)(2,1)S(1)} %copy-done.13, ...), custom_call_target="tpu_custom_call" | custom-call | flops 6039797760 | bytes 3145728 | tf_op jit(solution)/shard_map/attention_backward/pallas_call | solution.py:125
  148.4 9.2 %convolution_convert_fusion = bf16[2048,2048]{1,0:T(8,128)(2,1)} fusion(bf16[2048,768]{1,0:T(8,128)(2,1)S(1)} %attention_forward.1, bf16[768,2048]{1,0:T(8,128)(2,1)S(1)} %constant_dynamic-update-slice_fusion), kind=kOutput, calls=%fused_computation | convolution fusion | flops 6446645248 | bytes 14680064 | tf_op jit(solution)/shard_map/dot_general | solution.py:472
  157.6 6.7 %collective-permute-done.15.rest_0_ = bf16[384,512]{1,0:T(8,128)(2,1)S(1)} collective-permute-done((bf16[384,512]{1,0:T(8,128)(2,1)S(1)}, bf16[384,512]{1,0:T(8,128)(2,1)S(1)}, u32[]{:S(2)}, u32[]{:S(2)}) %collective-permute-start.15) | collective-permute-done | bytes 393248 | tf_op jit(solution)/shard_map/ppermute | solution.py:371
  164.3 4.0 %collective-permute-done.19.rest_0_ = bf16[384,512]{1,0:T(8,128)(2,1)S(1)} collective-permute-done((bf16[384,512]{1,0:T(8,128)(2,1)S(1)}, bf16[384,512]{1,0:T(8,128)(2,1)S(1)}, u32[]{:S(2)}, u32[]{:S(2)}) %collective-permute-start.19) | collective-permute-done | bytes 393248 | tf_op jit(solution)/shard_map/ppermute | solution.py:371
  170.2 2.1 collective-permute-start.22
  172.7 3.5 %collective-permute-start.24 = (bf16[192,512]{1,0:T(8,128)(2,1)S(1)}, bf16[192,512]{1,0:T(8,128)(2,1)S(1)}, u32[]{:S(2)}, u32[]{:S(2)}) collective-permute-start(bf16[192,512]{1,0:T(8,128)(2,1)S(1)} %slice.47), channel_id=1, source_target_pairs={{0,12},{4,0},{8,4},{12,8},{1,13},{5,1},{9,5},{13,9},{2,14},{6,2},{... | collective-permute-start | bytes 589832 | tf_op jit(solution)/shard_map/ppermute | solution.py:371
  176.1 6.4 %attention_backward.5 = (bf16[768,2048]{1,0:T(8,128)(2,1)S(1)}, f32[768,256]{1,0:T(8,128)S(1)}, f32[768,256]{1,0:T(8,128)S(1)}) custom-call(s32[20]{0:T(128)S(1)} %stack.82.place_ref, bf16[768,2048]{1,0:T(8,128)(2,1)S(1)} %select_dynamic-update-slice_fusion.q_ref, ...), custom_call_target="tpu_custom_call", output_to_operand_aliasing={{0}: (6, {}), {1}: (7, {}), {2}: (8, {})} | custom-call | flops 6039797760 | bytes 3145728 | tf_op jit(solution)/shard_map/attention_backward/pallas_call | solution.py:125
  182.5 6.4 %attention_backward.6 = (bf16[768,2048]{1,0:T(8,128)(2,1)S(1)}, f32[768,256]{1,0:T(8,128)S(1)}, f32[768,256]{1,0:T(8,128)S(1)}) custom-call(s32[20]{0:T(128)S(1)} %stack.82.place_ref, bf16[768,2048]{1,0:T(8,128)(2,1)S(1)} %select_dynamic-update-slice_fusion.q_ref, ...), custom_call_target="tpu_custom_call", output_to_operand_aliasing={{0}: (6, {}), {1}: (7, {}), {2}: (8, {})} | custom-call | flops 6039797760 | bytes 3145728 | tf_op jit(solution)/shard_map/attention_backward/pallas_call | solution.py:125
  189.0 6.4 %attention_backward.7 = (bf16[768,2048]{1,0:T(8,128)(2,1)S(1)}, f32[768,256]{1,0:T(8,128)S(1)}, f32[768,256]{1,0:T(8,128)S(1)}) custom-call(s32[20]{0:T(128)S(1)} %stack.82.place_ref, bf16[768,2048]{1,0:T(8,128)(2,1)S(1)} %select_dynamic-update-slice_fusion.q_ref, ...), custom_call_target="tpu_custom_call", output_to_operand_aliasing={{0}: (8, {}), {1}: (9, {}), {2}: (10, {})} | custom-call | flops 6039797760 | bytes 3145728 | tf_op jit(solution)/shard_map/attention_backward/pallas_call | solution.py:125
  195.5 5.7 %input_gradients.2 = (bf16[192,2048]{1,0:T(8,128)(2,1)S(1)}, bf16[192,2048]{1,0:T(8,128)(2,1)S(1)}) custom-call(s32[20]{0:T(128)S(1)} %stack.82.place_ref, bf16[768,2048]{1,0:T(8,128)(2,1)S(1)} %get-tuple-element.178.dq_ref, f32[768,256]{1,0:T(8,128)S(1)} %get-tuple-element.179.dk_ref, f32[768,256]{1,0:T(8,128)S(1)} %get-tuple-element.180.dv_ref, ...), custom_call_target="tpu_custom_call" | custom-call | flops 4026531840 | bytes 15990784 | tf_op jit(solution)/shard_map/input_gradients/pallas_call | solution.py:227
  201.2 2.3 collective-permute-done.25
  204.7 5.7 %input_gradients.3 = (bf16[192,2048]{1,0:T(8,128)(2,1)S(1)}, bf16[192,2048]{1,0:T(8,128)(2,1)S(1)}) custom-call(s32[20]{0:T(128)S(1)} %stack.82.place_ref, bf16[768,2048]{1,0:T(8,128)(2,1)S(1)} %get-tuple-element.178.dq_ref, f32[768,256]{1,0:T(8,128)S(1)} %get-tuple-element.179.dk_ref, f32[768,256]{1,0:T(8,128)S(1)} %get-tuple-element.180.dv_ref, ...), custom_call_target="tpu_custom_call" | custom-call | flops 4026531840 | bytes 15990784 | tf_op jit(solution)/shard_map/input_gradients/pallas_call | solution.py:227
  217.2 10.3 %weight_gradients.1 = (bf16[2048,2048]{1,0:T(8,128)(2,1)}, bf16[2048,256]{1,0:T(8,128)(2,1)}, bf16[2048,256]{1,0:T(8,128)(2,1)}) custom-call(bf16[768,2048]{1,0:T(8,128)(2,1)S(1)} %copy-done.20, bf16[768,2048]{1,0:T(8,128)(2,1)S(1)} %copy-done.1, f32[768,256]{1,0:T(8,128)S(1)} %copy-done.5, f32[768,256]{1,0:T(8,128)S(1)} %copy-done.7), custom_call_target="tpu_custom_call" | custom-call | flops 8053063680 | bytes 16777216 | tf_op jit(solution)/shard_map/weight_gradients/pallas_call | solution.py:195
  227.5 3.2 %collective-permute-done.26 = bf16[192,2048]{1,0:T(8,128)(2,1)} collective-permute-done((bf16[192,2048]{1,0:T(8,128)(2,1)}, bf16[192,2048]{1,0:T(8,128)(2,1)}, u32[]{:S(2)}, u32[]{:S(2)}) %collective-permute-start.26) | collective-permute-done | bytes 786464 | tf_op jit(solution)/shard_map/ppermute | solution.py:367
  230.7 2.6 %add_convert_fusion = bf16[192,2048]{1,0:T(8,128)(2,1)} fusion(bf16[192,2048]{1,0:T(8,128)(2,1)} %collective-permute-done.26, bf16[192,2048]{1,0:T(8,128)(2,1)} %collective-permute-done.27, bf16[192,2048]{1,0:T(8,128)(2,1)S(1)} %get-tuple-element.184), kind=kLoop, calls=%fused_computation.1 | loop fusion | flops 2359296 | bytes 3145728 | tf_op jit(solution)/shard_map/convert_element_type | solution.py:493
  (116 shorter events, 34.2 us)
Async XLA Ops:
  7.2 204.0 %all-gather.2.cloned.1.call-start = ((), (), s32[]{:S(2)}) async-start(), calls=%async_computation | async-start | bytes 3932160 | tf_op jit(solution)/shard_map/all_gather | solution.py:428
  7.2 8.9 %collective-permute-start.6 = (bf16[192,2048]{1,0:T(8,128)(2,1)}, bf16[192,2048]{1,0:T(8,128)(2,1)S(1)}, u32[]{:S(2)}, u32[]{:S(2)}) collective-permute-start(bf16[192,2048]{1,0:T(8,128)(2,1)} %first_ref.1), channel_id=1, source_target_pairs={{0,1},{1,0},{2,3},{3,2},{4,5},{5,4},{6,7},{7,6},{8,9},{9,8},{10,11... | collective-permute-start | bytes 2359304 | tf_op jit(solution)/shard_map/ppermute | solution.py:367
  7.7 21.0 %collective-permute-start.7 = (bf16[192,2048]{1,0:T(8,128)(2,1)}, bf16[192,2048]{1,0:T(8,128)(2,1)}, u32[]{:S(2)}, u32[]{:S(2)}) collective-permute-start(bf16[192,2048]{1,0:T(8,128)(2,1)} %first_ref.1), channel_id=1, source_target_pairs={{0,2},{2,0},{1,3},{3,1},{4,6},{6,4},{5,7},{7,5},{8,10},{10,8},{9,1... | collective-permute-start | bytes 2359304 | tf_op jit(solution)/shard_map/ppermute | solution.py:367
  10.3 20.9 %collective-permute-start = (bf16[192,2048]{1,0:T(8,128)(2,1)}, bf16[192,2048]{1,0:T(8,128)(2,1)}, u32[]{:S(2)}, u32[]{:S(2)}) collective-permute-start(bf16[192,2048]{1,0:T(8,128)(2,1)} %param.10), channel_id=1, source_target_pairs={{0,4},{4,8},{8,12},{1,5},{5,9},{9,13},{2,6},{6,10},{10,14},{3,7},{... | collective-permute-start | bytes 2359304 | tf_op jit(solution)/shard_map/ppermute | solution.py:376
  14.7 21.5 %collective-permute-start.3 = (bf16[192,2048]{1,0:T(8,128)(2,1)}, bf16[192,2048]{1,0:T(8,128)(2,1)}, u32[]{:S(2)}, u32[]{:S(2)}) collective-permute-start(bf16[192,2048]{1,0:T(8,128)(2,1)} %param.10), channel_id=1, source_target_pairs={{4,0},{8,4},{12,8},{5,1},{9,5},{13,9},{6,2},{10,6},{14,10},{7,3},{... | collective-permute-start | bytes 2359304 | tf_op jit(solution)/shard_map/ppermute | solution.py:376
  28.7 13.5 %collective-permute-start.8 = (bf16[192,2048]{1,0:T(8,128)(2,1)}, bf16[192,2048]{1,0:T(8,128)(2,1)}, u32[]{:S(2)}, u32[]{:S(2)}) collective-permute-start(bf16[192,2048]{1,0:T(8,128)(2,1)} %collective-permute-done.7.first_ref), channel_id=1, source_target_pairs={{0,1},{1,0},{2,3},{3,2},{4,5},{5,4},{6,7},{7,6},{8,9},{9,8},{10,11... | collective-permute-start | bytes 2359304 | tf_op jit(solution)/shard_map/ppermute | solution.py:367
  31.2 40.9 %collective-permute-start.1 = (bf16[192,2048]{1,0:T(8,128)(2,1)}, bf16[192,2048]{1,0:T(8,128)(2,1)}, u32[]{:S(2)}, u32[]{:S(2)}) collective-permute-start(bf16[192,2048]{1,0:T(8,128)(2,1)} %collective-permute-done), channel_id=1, source_target_pairs={{4,8},{8,12},{5,9},{9,13},{6,10},{10,14},{7,11},{11,15},{20,24},{2... | collective-permute-start | bytes 2359304 | tf_op jit(solution)/shard_map/ppermute | solution.py:376
  36.2 36.6 %collective-permute-start.4 = (bf16[192,2048]{1,0:T(8,128)(2,1)}, bf16[192,2048]{1,0:T(8,128)(2,1)}, u32[]{:S(2)}, u32[]{:S(2)}) collective-permute-start(bf16[192,2048]{1,0:T(8,128)(2,1)} %collective-permute-done.3), channel_id=1, source_target_pairs={{4,0},{8,4},{5,1},{9,5},{6,2},{10,6},{7,3},{11,7},{20,16},{24,20},... | collective-permute-start | bytes 2359304 | tf_op jit(solution)/shard_map/ppermute | solution.py:376
  39.4 30.2 %copy-start.15 = (bf16[384,512]{1,0:T(8,128)(2,1)S(1)}, bf16[384,512]{1,0:T(8,128)(2,1)}, u32[]{:S(2)}) copy-start(bf16[384,512]{1,0:T(8,128)(2,1)} %copy-done.14) | copy-start | bytes 1179652
  39.4 30.2 %collective-permute-start.10 = (bf16[192,512]{1,0:T(8,128)(2,1)}, bf16[192,512]{1,0:T(8,128)(2,1)S(1)}, u32[]{:S(2)}, u32[]{:S(2)}) collective-permute-start(bf16[192,512]{1,0:T(8,128)(2,1)} %copy-done.22), channel_id=1, source_target_pairs={{0,12},{4,0},{8,4},{12,8},{1,13},{5,1},{9,5},{13,9},{2,14},{6,2},{... | collective-permute-start | bytes 589832 | tf_op jit(solution)/shard_map/ppermute | solution.py:371
  40.6 29.1 %collective-permute-start.9 = (bf16[192,512]{1,0:T(8,128)(2,1)}, bf16[192,512]{1,0:T(8,128)(2,1)S(1)}, u32[]{:S(2)}, u32[]{:S(2)}) collective-permute-start(bf16[192,512]{1,0:T(8,128)(2,1)} %copy-done.21), channel_id=1, source_target_pairs={{0,4},{4,8},{8,12},{12,0},{1,5},{5,9},{9,13},{13,1},{2,6},{6,10},{... | collective-permute-start | bytes 589832 | tf_op jit(solution)/shard_map/ppermute | solution.py:371
  52.0 22.2 %collective-permute-start.11 = (bf16[192,512]{1,0:T(8,128)(2,1)S(1)}, bf16[192,512]{1,0:T(8,128)(2,1)S(1)}, u32[]{:S(2)}, u32[]{:S(2)}) collective-permute-start(bf16[192,512]{1,0:T(8,128)(2,1)S(1)} %get-tuple-element.106), channel_id=1, source_target_pairs={{0,4},{4,8},{8,12},{12,0},{1,5},{5,9},{9,13},{13,1},{2,6},{6,10},{... | collective-permute-start | bytes 589832 | tf_op jit(solution)/shard_map/ppermute | solution.py:371
  69.6 7.8 %collective-permute-start.12 = (bf16[192,512]{1,0:T(8,128)(2,1)S(1)}, bf16[192,512]{1,0:T(8,128)(2,1)S(1)}, u32[]{:S(2)}, u32[]{:S(2)}) collective-permute-start(bf16[192,512]{1,0:T(8,128)(2,1)S(1)} %get-tuple-element.105), channel_id=1, source_target_pairs={{0,12},{4,0},{8,4},{12,8},{1,13},{5,1},{9,5},{13,9},{2,14},{6,2},{... | collective-permute-start | bytes 589832 | tf_op jit(solution)/shard_map/ppermute | solution.py:371
  69.8 64.3 %collective-permute-start.14 = (bf16[384,512]{1,0:T(8,128)(2,1)S(1)}, bf16[384,512]{1,0:T(8,128)(2,1)S(1)}, u32[]{:S(2)}, u32[]{:S(2)}) collective-permute-start(bf16[384,512]{1,0:T(8,128)(2,1)S(1)} %pad_maximum_fusion.1), channel_id=1, source_target_pairs={{0,12},{4,0},{8,4},{12,8},{1,13},{5,1},{9,5},{13,9},{2,14},{6,2},{... | collective-permute-start | bytes 1179656 | tf_op jit(solution)/shard_map/ppermute | solution.py:371
  72.1 7.6 %collective-permute-start.2 = (bf16[192,2048]{1,0:T(8,128)(2,1)}, bf16[192,2048]{1,0:T(8,128)(2,1)S(1)}, u32[]{:S(2)}, u32[]{:S(2)}) collective-permute-start(bf16[192,2048]{1,0:T(8,128)(2,1)} %collective-permute-done.1), channel_id=1, source_target_pairs={{8,12},{9,13},{10,14},{11,15},{24,28},{25,29},{26,30},{27,31}} | collective-permute-start | bytes 2359304 | tf_op jit(solution)/shard_map/ppermute | solution.py:376
  72.8 38.4 %collective-permute-start.5 = (bf16[192,2048]{1,0:T(8,128)(2,1)}, bf16[192,2048]{1,0:T(8,128)(2,1)S(1)}, u32[]{:S(2)}, u32[]{:S(2)}) collective-permute-start(bf16[192,2048]{1,0:T(8,128)(2,1)} %collective-permute-done.4), channel_id=1, source_target_pairs={{4,0},{5,1},{6,2},{7,3},{20,16},{21,17},{22,18},{23,19}} | collective-permute-start | bytes 2359304 | tf_op jit(solution)/shard_map/ppermute | solution.py:376
  74.1 37.4 %copy-start.9 = (bf16[192,2048]{1,0:T(8,128)(2,1)S(1)}, bf16[192,2048]{1,0:T(8,128)(2,1)}, u32[]{:S(2)}) copy-start(bf16[192,2048]{1,0:T(8,128)(2,1)} %first_ref.1) | copy-start | bytes 2359300
  74.2 59.9 %collective-permute-start.13 = (bf16[384,512]{1,0:T(8,128)(2,1)S(1)}, bf16[384,512]{1,0:T(8,128)(2,1)S(1)}, u32[]{:S(2)}, u32[]{:S(2)}) collective-permute-start(bf16[384,512]{1,0:T(8,128)(2,1)S(1)} %pad_maximum_fusion), channel_id=1, source_target_pairs={{0,4},{4,8},{8,12},{12,0},{1,5},{5,9},{9,13},{13,1},{2,6},{6,10},{... | collective-permute-start | bytes 1179656 | tf_op jit(solution)/shard_map/ppermute | solution.py:371
  77.5 34.1 %copy-start.11 = (bf16[192,2048]{1,0:T(8,128)(2,1)S(1)}, bf16[192,2048]{1,0:T(8,128)(2,1)}, u32[]{:S(2)}) copy-start(bf16[192,2048]{1,0:T(8,128)(2,1)} %copy-done.10) | copy-start | bytes 2359300
  77.6 56.7 %collective-permute-start.17 = (bf16[384,512]{1,0:T(8,128)(2,1)S(1)}, bf16[384,512]{1,0:T(8,128)(2,1)S(1)}, u32[]{:S(2)}, u32[]{:S(2)}) collective-permute-start(bf16[384,512]{1,0:T(8,128)(2,1)S(1)} %pad_maximum_fusion.3), channel_id=1, source_target_pairs={{0,12},{4,0},{8,4},{12,8},{1,13},{5,1},{9,5},{13,9},{2,14},{6,2},{... | collective-permute-start | bytes 1179656 | tf_op jit(solution)/shard_map/ppermute | solution.py:371
  79.7 54.6 %collective-permute-start.16 = (bf16[384,512]{1,0:T(8,128)(2,1)S(1)}, bf16[384,512]{1,0:T(8,128)(2,1)S(1)}, u32[]{:S(2)}, u32[]{:S(2)}) collective-permute-start(bf16[384,512]{1,0:T(8,128)(2,1)S(1)} %pad_maximum_fusion.2), channel_id=1, source_target_pairs={{0,4},{4,8},{8,12},{12,0},{1,5},{5,9},{9,13},{13,1},{2,6},{6,10},{... | collective-permute-start | bytes 1179656 | tf_op jit(solution)/shard_map/ppermute | solution.py:371
  134.4 23.2 %collective-permute-start.18 = (bf16[384,512]{1,0:T(8,128)(2,1)S(1)}, bf16[384,512]{1,0:T(8,128)(2,1)S(1)}, u32[]{:S(2)}, u32[]{:S(2)}) collective-permute-start(bf16[384,512]{1,0:T(8,128)(2,1)S(1)} %add_convert_fusion.1.rest_1_), channel_id=1, source_target_pairs={{0,4},{4,8},{8,12},{12,0},{1,5},{5,9},{9,13},{13,1},{2,6},{6,10},{... | collective-permute-start | bytes 1179656 | tf_op jit(solution)/shard_map/ppermute | solution.py:371
  135.3 22.3 %collective-permute-start.20 = (bf16[384,512]{1,0:T(8,128)(2,1)S(1)}, bf16[384,512]{1,0:T(8,128)(2,1)S(1)}, u32[]{:S(2)}, u32[]{:S(2)}) collective-permute-start(bf16[384,512]{1,0:T(8,128)(2,1)S(1)} %add_convert_fusion.1.rest_1_), channel_id=1, source_target_pairs={{0,12},{4,0},{8,4},{12,8},{1,13},{5,1},{9,5},{13,9},{2,14},{6,2},{... | collective-permute-start | bytes 1179656 | tf_op jit(solution)/shard_map/ppermute | solution.py:371
  138.3 26.0 %collective-permute-start.15 = (bf16[384,512]{1,0:T(8,128)(2,1)S(1)}, bf16[384,512]{1,0:T(8,128)(2,1)S(1)}, u32[]{:S(2)}, u32[]{:S(2)}) collective-permute-start(bf16[384,512]{1,0:T(8,128)(2,1)S(1)} %add_convert_fusion.2.rest_0_), channel_id=1, source_target_pairs={{0,4},{4,8},{8,12},{12,0},{1,5},{5,9},{9,13},{13,1},{2,6},{6,10},{... | collective-permute-start | bytes 1179656 | tf_op jit(solution)/shard_map/ppermute | solution.py:371
  138.3 30.0 %collective-permute-start.19 = (bf16[384,512]{1,0:T(8,128)(2,1)S(1)}, bf16[384,512]{1,0:T(8,128)(2,1)S(1)}, u32[]{:S(2)}, u32[]{:S(2)}) collective-permute-start(bf16[384,512]{1,0:T(8,128)(2,1)S(1)} %add_convert_fusion.2.rest_0_), channel_id=1, source_target_pairs={{0,12},{4,0},{8,4},{12,8},{1,13},{5,1},{9,5},{13,9},{2,14},{6,2},{... | collective-permute-start | bytes 1179656 | tf_op jit(solution)/shard_map/ppermute | solution.py:371
  168.4 20.5 %collective-permute-start.21 = (bf16[192,512]{1,0:T(8,128)(2,1)S(1)}, bf16[192,512]{1,0:T(8,128)(2,1)S(1)}, u32[]{:S(2)}, u32[]{:S(2)}) collective-permute-start(bf16[192,512]{1,0:T(8,128)(2,1)S(1)} %slice.44), channel_id=1, source_target_pairs={{0,4},{4,8},{8,12},{12,0},{1,5},{5,9},{9,13},{13,1},{2,6},{6,10},{... | collective-permute-start | bytes 589832 | tf_op jit(solution)/shard_map/ppermute | solution.py:371
  170.2 18.8 %collective-permute-start.22 = (bf16[192,512]{1,0:T(8,128)(2,1)S(1)}, bf16[192,512]{1,0:T(8,128)(2,1)S(1)}, u32[]{:S(2)}, u32[]{:S(2)}) collective-permute-start(bf16[192,512]{1,0:T(8,128)(2,1)S(1)} %slice.45), channel_id=1, source_target_pairs={{0,12},{4,0},{8,4},{12,8},{1,13},{5,1},{9,5},{13,9},{2,14},{6,2},{... | collective-permute-start | bytes 589832 | tf_op jit(solution)/shard_map/ppermute | solution.py:371
  172.3 16.7 %collective-permute-start.23 = (bf16[192,512]{1,0:T(8,128)(2,1)S(1)}, bf16[192,512]{1,0:T(8,128)(2,1)S(1)}, u32[]{:S(2)}, u32[]{:S(2)}) collective-permute-start(bf16[192,512]{1,0:T(8,128)(2,1)S(1)} %slice.46), channel_id=1, source_target_pairs={{0,4},{4,8},{8,12},{12,0},{1,5},{5,9},{9,13},{13,1},{2,6},{6,10},{... | collective-permute-start | bytes 589832 | tf_op jit(solution)/shard_map/ppermute | solution.py:371
  172.7 16.3 %collective-permute-start.24 = (bf16[192,512]{1,0:T(8,128)(2,1)S(1)}, bf16[192,512]{1,0:T(8,128)(2,1)S(1)}, u32[]{:S(2)}, u32[]{:S(2)}) collective-permute-start(bf16[192,512]{1,0:T(8,128)(2,1)S(1)} %slice.47), channel_id=1, source_target_pairs={{0,12},{4,0},{8,4},{12,8},{1,13},{5,1},{9,5},{13,9},{2,14},{6,2},{... | collective-permute-start | bytes 589832 | tf_op jit(solution)/shard_map/ppermute | solution.py:371
  201.2 2.4 collective-permute-start.25
  210.4 17.1 %collective-permute-start.27 = (bf16[192,2048]{1,0:T(8,128)(2,1)S(1)}, bf16[192,2048]{1,0:T(8,128)(2,1)}, u32[]{:S(2)}, u32[]{:S(2)}) collective-permute-start(bf16[192,2048]{1,0:T(8,128)(2,1)S(1)} %get-tuple-element.185), channel_id=1, source_target_pairs={{0,1},{1,0},{2,3},{3,2},{4,5},{5,4},{6,7},{7,6},{8,9},{9,8},{10,11... | collective-permute-start | bytes 2359304 | tf_op jit(solution)/shard_map/ppermute | solution.py:367
  210.6 20.1 %collective-permute-start.26 = (bf16[192,2048]{1,0:T(8,128)(2,1)}, bf16[192,2048]{1,0:T(8,128)(2,1)}, u32[]{:S(2)}, u32[]{:S(2)}) collective-permute-start(bf16[192,2048]{1,0:T(8,128)(2,1)} %add.115), channel_id=1, source_target_pairs={{0,2},{2,0},{1,3},{3,1},{4,6},{6,4},{5,7},{7,5},{8,10},{10,8},{9,1... | collective-permute-start | bytes 2359304 | tf_op jit(solution)/shard_map/ppermute | solution.py:367
  (22 other events, 137.4 us)
Sparse Core Ops, SparseCore 0:
  28.9 30.1 all-gather.1

commit v2 on v0

--- a/solution.py
+++ b/solution.py
@@ -1,13 +1,318 @@
+import functools
+
 import jax
 import jax.numpy as jnp
 from jax import lax
+from jax.experimental import pallas as pl
+from jax.experimental.pallas import tpu as pltpu
 from jax.sharding import PartitionSpec as P
 
 QUERY_HEADS = 64
 KEY_VALUE_HEADS = 8
 HEAD_SIZE = 128
 SEQUENCE_LENGTH = 256
-
+SCALE = HEAD_SIZE ** (-0.5)
+LOG2E = 1.4426950408889634
+F32 = jnp.float32
+BF = jnp.bfloat16
+PLACE_SEND, PLACE_HEAD, PLACE_KEY, PLACE_BLOCK, PLACE_HALF, PLACE_SUB, PLACE_END, PLACE_PART, PLACE_TURN = 0, 4, 8, 12, 16, 18, 20, 21, 25
+SEND_ORDER = ((3, 2, 1, 0), (3, 2, 0, 1), (0, 1, 3, 2), (0, 1, 2, 3))
+TURN_ORDER = ((0, 1, 2), (0, 1, 2), (2, 1, 0), (2, 1, 0))
+HEAD_ORDER = ((0, 1, 2, 3), (1, 0, 2, 3), (2, 3, 1, 0), (3, 2, 1, 0))
+BLOCK = 128
+GROUP = 4
+COST = pl.CostEstimate(flops=1 << 20, bytes_accessed=1 << 16, transcendentals=0)
+STREAMED = pltpu.CompilerParams(vmem_limit_bytes=60 * 1024 * 1024)
+PARAMS = pltpu.CompilerParams(vmem_limit_bytes=24 * 1024 * 1024)
+SMALL = pltpu.CompilerParams(vmem_limit_bytes=12 * 1024 * 1024)
+CONTRACT_LAST = (((1,), (1,)), ((), ()))
+
+def probabilities(keys, stacked, start):
+    scores = lax.dot_general(keys, stacked, CONTRACT_LAST, preferred_element_type=F32)
+    shape = (BLOCK, stacked.shape[0])
+    allowed = lax.broadcasted_iota(jnp.int32, shape, 0) <= lax.broadcasted_iota(jnp.int32, shape, 1) % BLOCK
+    diagonal = jnp.where(allowed, scores[start:], -jnp.inf)
+    scores = jnp.concatenate([scores[:start], diagonal]) if start else diagonal
+    top = jnp.max(scores, axis=0, keepdims=True)
+    raised = jnp.exp2((scores - top) * (SCALE * LOG2E))
+    total = jnp.sum(raised, axis=0, keepdims=True)
+    return raised * (1.0 / total)
+
+
+def stack(ref, rows, heads):
+    return jnp.concatenate([ref[rows, h * HEAD_SIZE : (h + 1) * HEAD_SIZE] for h in range(heads)])
+
+
+def assemble(place_ref, refs, groups, whole_ref):
+    rows = whole_ref.shape[0] // 4
+
+    def put(ref, at):
+        whole_ref[pl.ds(pl.multiple_of(place_ref[PLACE_PART + at], 64), rows), :] = ref[...]
+
+    first = 0
+    for at, count in enumerate(groups):
+        if count == 1:
+            put(refs[first], at)
+        else:
+            for choice in range(2):
+                pl.when(place_ref[PLACE_END] == 1 - choice)(functools.partial(put, refs[first + choice], at))
+        first += count
+
+
+def forward_kernel(groups, turn, earlier, place_ref, *refs):
+    parts, refs = refs[: sum(groups)], refs[sum(groups) :]
+    k_ref, v_ref = refs[:2]
+    o_ref, whole_ref = refs[2 + earlier :]
+    step = pl.program_id(1)
+    heads = whole_ref.shape[1] // HEAD_SIZE
+
+    @pl.when(step == 0)
+    def _():
+        assemble(place_ref, parts, groups, whole_ref)
+
+    keys = k_ref[...]
+    values_t = v_ref[...].T
+    base = place_ref[PLACE_TURN + turn + step] * SEQUENCE_LENGTH
+    for start in range(0, SEQUENCE_LENGTH, BLOCK):
+        stop = start + BLOCK
+        here = pl.ds(pl.multiple_of(base + start, BLOCK), BLOCK)
+        for first in range(0, heads, GROUP):
+            stacked = jnp.concatenate(
+                [whole_ref[here, h * HEAD_SIZE : (h + 1) * HEAD_SIZE] for h in range(first, first + GROUP)]
+            )
+            soft = probabilities(keys[:stop], stacked, start).astype(BF)
+            attended = jnp.dot(values_t[:, :stop], soft, preferred_element_type=F32).astype(BF)
+            for n in range(GROUP):
+                h = first + n
+                o_ref[h * HEAD_SIZE : (h + 1) * HEAD_SIZE, start:stop] = attended[:, n * BLOCK : (n + 1) * BLOCK]
+
+
+def attended_transposed(place, parts, keys, values, turn, count, earlier=()):
+    flat = [x for part in parts for x in part]
+    rows, width = flat[0].shape
+    tokens = keys.shape[0]
+    kv = keys.shape[1] // HEAD_SIZE
+    each = width // kv
+    L = SEQUENCE_LENGTH
+    small = pl.BlockSpec((L, HEAD_SIZE), lambda g, s, place: (place[PLACE_TURN + turn + s], g))
+    spec = pltpu.PrefetchScalarGridSpec(
+        num_scalar_prefetch=1,
+        grid=(kv, count),
+        in_specs=[pl.BlockSpec((rows, each), lambda g, s, place: (0, g))] * len(flat)
+        + [small, small]
+        + [pl.BlockSpec(memory_space=pl.ANY)] * len(earlier),
+        out_specs=pl.BlockSpec((each, L), lambda g, s, place: (g, place[PLACE_TURN + turn + s])),
+        scratch_shapes=[pltpu.VMEM((4 * rows, each), BF)],
+    )
+    return pl.pallas_call(
+        functools.partial(forward_kernel, [len(part) for part in parts], turn, len(earlier)),
+        grid_spec=spec,
+        out_shape=jax.ShapeDtypeStruct((width, tokens), BF),
+        input_output_aliases={3 + len(flat): 0} if earlier else {},
+        compiler_params=SMALL,
+        name="attention_forward",
+        cost_estimate=COST,
+    )(place, *flat, keys, values, *earlier)
+
+
+def backward_kernel(slot, heads, groups, counts, place_ref, k_ref, v_ref, *rest):
+    parts, rest = rest[: sum(counts)], rest[sum(counts) :]
+    pieces, rest = rest[: sum(groups)], rest[sum(groups) :]
+    if slot == 0:
+        dq_ref, dk_ref, dv_ref, grad_ref, q_ref = rest
+    else:
+        _, dk_in, dv_in, dq_ref, dk_ref, dv_ref, grad_ref, q_ref = rest
+    s = pl.program_id(0)
+    L = SEQUENCE_LENGTH
+    rows = grad_ref.shape[0] // 4
+
+    def put(ref, chunk):
+        for j in range(2):
+            offset = pl.multiple_of(place_ref[PLACE_BLOCK + 2 * chunk + j], 64)
+            grad_ref[pl.ds(offset, rows), :] = ref[j * rows : (j + 1) * rows, :]
+
+    @pl.when(s == 0)
+    def _():
+        assemble(place_ref, parts, counts, q_ref)
+        at = 0
+        for chunk, count in enumerate(groups):
+            if count == 1:
+                put(pieces[at], chunk)
+            else:
+                for choice in range(2):
+                    pl.when(place_ref[PLACE_END] == 1 - choice)(functools.partial(put, pieces[at + choice], chunk))
+            at += count
+
+    keys = k_ref[...]
+    values = v_ref[...]
+    keys_t = keys.T
+    dk_ref[...] = dk_in[...] if slot % 2 else jnp.zeros((L, HEAD_SIZE), F32)
+    dv_ref[...] = dv_in[...] if slot % 2 else jnp.zeros((L, HEAD_SIZE), F32)
+    for start in range(0, L, BLOCK):
+        stop = start + BLOCK
+        here = pl.ds(pl.multiple_of(s * L + start, BLOCK), BLOCK)
+        stacked = stack(q_ref, here, heads)
+        grads = stack(grad_ref, here, heads)
+        soft = probabilities(keys[:stop], stacked, start)
+        soft_grad = lax.dot_general(values[:stop], grads, CONTRACT_LAST, preferred_element_type=F32)
+        dots = jnp.sum(soft * soft_grad, axis=0, keepdims=True)
+        score_grad = (soft * (soft_grad - dots)).astype(BF)
+        dv_ref[:stop, :] += jnp.dot(soft.astype(BF), grads, preferred_element_type=F32)
+        dk_ref[:stop, :] += jnp.dot(score_grad, stacked, preferred_element_type=F32) * SCALE
+        dq_t = (jnp.dot(keys_t[:, :stop], score_grad, preferred_element_type=F32) * SCALE).astype(BF)
+        for h in range(heads):
+            dq_ref[start:stop, h * HEAD_SIZE : (h + 1) * HEAD_SIZE] = dq_t[:, h * BLOCK : (h + 1) * BLOCK].T
+
+
+def attention_backward(slot, place, parts, keys, values, chunks, earlier):
+    flat = [x for part in parts for x in part]
+    pieces = [piece for chunk in chunks for piece in chunk]
+    rows, width = flat[0].shape
+    tokens = keys.shape[0]
+    quarter = pieces[0].shape[1]
+    L = SEQUENCE_LENGTH
+    small = pl.BlockSpec((L, HEAD_SIZE), lambda s, place: (s, place[PLACE_KEY + slot]))
+    wide = pl.BlockSpec((L, quarter), lambda s, place: (s, place[PLACE_HEAD + slot]))
+    n = len(pieces) + len(flat)
+    spec = pltpu.PrefetchScalarGridSpec(
+        num_scalar_prefetch=1,
+        grid=(tokens // L,),
+        in_specs=[small, small]
+        + [pl.BlockSpec((rows, quarter), lambda s, place: (0, place[PLACE_HEAD + slot]))] * len(flat)
+        + [pl.BlockSpec(x.shape, lambda s, place: (0, 0)) for x in pieces]
+        + ([] if slot == 0 else [pl.BlockSpec(memory_space=pl.ANY), small, small]),
+        out_specs=[wide, small, small],
+        scratch_shapes=[pltpu.VMEM((tokens, quarter), BF)] * 2,
+    )
+    sums = jax.ShapeDtypeStruct(keys.shape, F32)
+    return pl.pallas_call(
+        functools.partial(
+            backward_kernel,
+            slot,
+            quarter // HEAD_SIZE,
+            [len(chunk) for chunk in chunks],
+            [len(part) for part in parts],
+        ),
+        grid_spec=spec,
+        out_shape=[jax.ShapeDtypeStruct((tokens, width), BF), sums, sums],
+        input_output_aliases={} if slot == 0 else {3 + n: 0, 4 + n: 1, 5 + n: 2},
+        compiler_params=SMALL,
+        name="attention_backward",
+        cost_estimate=COST,
+    )(place, keys, values, *flat, *pieces, *([] if slot == 0 else earlier))
+
+
+def partial_kernel(place_ref, first_ref, second_ref, weight_ref, far_ref, near_ref, own_ref, both_ref):
+    step = pl.program_id(0)
+    rows = first_ref.shape[0]
+
+    @pl.when(step == 0)
+    def _():
+        both_ref[:rows, :] = first_ref[...]
+        both_ref[rows:, :] = second_ref[...]
+
+    product = lax.dot_general(both_ref[...], weight_ref[...], CONTRACT_LAST, preferred_element_type=F32).astype(BF)
+    for slot, (out_ref, at) in enumerate(((far_ref, 0), (near_ref, 0), (near_ref, 2 * rows), (own_ref, 0))):
+        @pl.when(step == slot)
+        def _(out_ref=out_ref, at=at):
+            out_ref[at : at + 2 * rows, :] = product
+
+
+def partial_products(place, first, second, weight):
+    rows, features = first.shape
+    quarter = weight.shape[0] // 4
+    shapes = [(2 * rows, quarter), (4 * rows, quarter), (2 * rows, quarter)]
+    same = lambda shape: pl.BlockSpec(shape, lambda k, place: (0, 0))
+    spec = pltpu.PrefetchScalarGridSpec(
+        num_scalar_prefetch=1,
+        grid=(4,),
+        in_specs=[
+            same(first.shape),
+            same(second.shape),
+            pl.BlockSpec((quarter, features), lambda k, place: (place[PLACE_SEND + k], 0)),
+        ],
+        out_specs=[same(shape) for shape in shapes],
+        scratch_shapes=[pltpu.VMEM((2 * rows, features), BF)],
+    )
+    return pl.pallas_call(
+        partial_kernel,
+        grid_spec=spec,
+        out_shape=[jax.ShapeDtypeStruct(shape, BF) for shape in shapes],
+        compiler_params=STREAMED,
+        name="gradient_partial",
+        cost_estimate=COST,
+    )(place, first, second, weight)
+
+
+def output_kernel(attended_ref, upstream_ref, out_ref):
+    out_ref[...] = jnp.dot(attended_ref[...], upstream_ref[...], preferred_element_type=F32).astype(BF)
+
+
+def output_gradient(attended, upstream, block=512):
+    width, tokens = attended.shape
+    features = upstream.shape[1]
+    return pl.pallas_call(
+        output_kernel,
+        grid=(width // block,),
+        in_specs=[pl.BlockSpec((block, tokens), lambda i: (i, 0)), pl.BlockSpec((tokens, features), lambda i: (0, 0))],
+        out_specs=pl.BlockSpec((block, features), lambda i: (i, 0)),
+        out_shape=jax.ShapeDtypeStruct((width, features), BF),
+        compiler_params=PARAMS,
+        name="output_gradient",
+        cost_estimate=COST,
+    )(attended, upstream)
+
+
+def weights_kernel(n_ref, dq_ref, dk_ref, dv_ref, gq_ref, gk_ref, gv_ref):
+    nt = n_ref[...].T
+    gq_ref[...] = jnp.dot(nt, dq_ref[...], preferred_element_type=F32).astype(BF)
+    gk_ref[...] = jnp.dot(nt, dk_ref[...].astype(BF), preferred_element_type=F32).astype(BF)
+    gv_ref[...] = jnp.dot(nt, dv_ref[...].astype(BF), preferred_element_type=F32).astype(BF)
+
+def weight_gradients(normed, dq, dk, dv, block=256):
+    tokens, feats = normed.shape
+    whole = lambda x: pl.BlockSpec(x.shape, lambda i:(0,0))
+    out = lambda x: pl.BlockSpec((block,x.shape[1]), lambda i:(i,0))
+    return pl.pallas_call(
+        weights_kernel, grid=(feats//block,),
+        in_specs=[pl.BlockSpec((tokens,block),lambda i:(0,i)),whole(dq),whole(dk),whole(dv)],
+        out_specs=[out(dq),out(dk),out(dv)],
+        out_shape=[jax.ShapeDtypeStruct((feats,x.shape[1]),BF) for x in (dq,dk,dv)],
+        compiler_params=STREAMED, name="weight_gradients",
+        cost_estimate=COST,
+    )(normed,dq,dk,dv)
+
+def input_kernel(half, place_ref, dq_ref, dk_ref, dv_ref, wq_ref, wk_ref, wv_ref, first_ref, second_ref, total_ref):
+    rows = first_ref.shape[0]
+    here = pl.ds(pl.multiple_of(place_ref[PLACE_HALF + half], 2 * rows), 2 * rows)
+    total = lax.dot_general(dq_ref[here, :], wq_ref[...], CONTRACT_LAST, preferred_element_type=F32)
+    total += lax.dot_general(dk_ref[here, :].astype(BF), wk_ref[...], CONTRACT_LAST, preferred_element_type=F32)
+    total += lax.dot_general(dv_ref[here, :].astype(BF), wv_ref[...], CONTRACT_LAST, preferred_element_type=F32)
+    total_ref[...] = total.astype(BF)
+    first_ref[...] = total_ref[pl.ds(pl.multiple_of(place_ref[PLACE_SUB], rows), rows), :]
+    second_ref[...] = total_ref[pl.ds(pl.multiple_of(place_ref[PLACE_SUB + 1], rows), rows), :]
+
+
+def input_gradients(half, place, rows, dq, dk, dv, query_weight, key_matrix, value_matrix, block=512):
+    features, width = query_weight.shape
+    small = key_matrix.shape[1]
+    whole = lambda x: pl.BlockSpec(x.shape, lambda i, place: (0, 0))
+    strip = lambda x: pl.BlockSpec((block, x.shape[1]), lambda i, place: (i, 0))
+    spec = pltpu.PrefetchScalarGridSpec(
+        num_scalar_prefetch=1,
+        grid=(features // block,),
+        in_specs=[whole(dq), whole(dk), whole(dv), strip(query_weight), strip(key_matrix), strip(value_matrix)],
+        out_specs=[pl.BlockSpec((rows, block), lambda i, place: (0, i))] * 2,
+        scratch_shapes=[pltpu.VMEM((2 * rows, block), BF)],
+    )
+    return pl.pallas_call(
+        functools.partial(input_kernel, half),
+        grid_spec=spec,
+        out_shape=[jax.ShapeDtypeStruct((rows, features), BF)] * 2,
+        compiler_params=PARAMS,
+        name="input_gradients",
+        cost_estimate=COST,
+    )(place, dq, dk, dv, query_weight, key_matrix, value_matrix)
 
 def attend(query_token_rows, key_token_rows, value_token_rows, gradient_rows):
     token_count = query_token_rows.shape[0]
@@ -62,7 +367,7 @@
     )
 
 
-def shards(
+def general_shards(
     normed,
     queries,
     stored_keys,
@@ -135,6 +440,158 @@
     return (grad_normed, grad_query, grad_key, grad_value, grad_output)
 
 
+def swap(x, axis):
+    return lax.ppermute(x, axis, [(0, 1), (1, 0)])
+
+
+def inward(x):
+    return lax.ppermute(x, "row", [(0, 1), (3, 2)])
+
+
+def across(x):
+    return lax.ppermute(x, "row", [(1, 2), (2, 1)])
+
+
+def outward(x):
+    return lax.ppermute(x, "row", [(1, 0), (2, 3)])
+
+
+def paired(x):
+    return lax.ppermute(x, "row", [(0, 1), (1, 0), (2, 3), (3, 2)])
+
+
+def after(value, others):
+    return lax.optimization_barrier((value, others))
+
+
+def plus(*terms):
+    return sum(term.astype(F32) for term in terms).astype(BF)
+
+
+def shards(
+    normed,
+    queries,
+    stored_keys,
+    stored_values,
+    upstream,
+    query_weight,
+    key_matrix,
+    value_matrix,
+    output_weight,
+):
+    row = lax.axis_index("row")
+    col = lax.axis_index("col")
+    sub = lax.axis_index("sub")
+    here = 2 * col + sub
+    rows = upstream.shape[0]
+    half = 2 * rows
+    is_end = (row == 0) | (row == 3)
+    index = jnp.arange(PLACE_TURN + 3, dtype=jnp.int32)
+    table = jnp.array(
+        [
+            SEND_ORDER[r]
+            + HEAD_ORDER[r]
+            + tuple(q // 2 for q in HEAD_ORDER[r])
+            + (0,) * 9
+            + tuple(rows * q for q in HEAD_ORDER[r])
+            + TURN_ORDER[r]
+            for r in range(4)
+        ]
+    )
+    place = jnp.sum(jnp.where(jnp.arange(4)[:, None] == row, table, 0), axis=0).astype(jnp.int32)
+    for at, value in enumerate(
+        [rows * (here ^ j) for j in range(4)]
+        + [half * (1 - col), half * col, rows * (1 - sub), rows * sub, is_end.astype(jnp.int32)]
+    ):
+        place = jnp.where(index == PLACE_BLOCK + at, value.astype(jnp.int32), place)
+
+    def backward(slot, pieces, results):
+        return attention_backward(slot, place, query_parts, stored_keys, stored_values, pieces, results)
+
+    first_up = swap(upstream, "sub")
+    query_pair = paired(queries)
+    second_up = swap(upstream, "col")
+    query_mid = across(queries)
+    a_far, a_near, a_own = partial_products(place, upstream, first_up, output_weight)
+    (query_pair, query_mid), a_far = after((query_pair, query_mid), a_far)
+    query_far = across(query_pair)
+    query_out = outward(query_mid)
+    (second_up, normed, late_upstream, a_far, a_near), (query_pair, query_mid) = after(
+        (second_up, normed, upstream, a_far, a_near), (query_pair, query_mid)
+    )
+    a_in0 = inward(a_far)
+    a_in = inward(a_near)
+    third_up = swap(second_up, "sub")
+    upstream_all = lax.all_gather(late_upstream, ("col", "sub"), axis=0, tiled=True)
+    normed_all = lax.all_gather(normed, ("col", "sub"), axis=0, tiled=True)
+    b_far, b_near, b_own = partial_products(place, second_up, third_up, output_weight)
+    b_in0 = inward(b_far)
+    a_in0, b_far = after(a_in0, b_far)
+    a_mid0 = across(plus(a_far, a_in0))
+    query_far, a_in0 = after(query_far, a_in0)
+    query_last = outward(query_far)
+
+    (a_mid0, query_out), query_far = after((a_mid0, query_out), query_far)
+    a_out = outward(plus(a_near[half:], a_mid0))
+    a_in, query_far = after(a_in, query_far)
+    a_mid1 = across(plus(a_near[:half], a_in[:half]))
+    b_in0, a_in = after(b_in0, a_in)
+    b_mid0 = across(plus(b_far, b_in0))
+    b_in = inward(b_near)
+    query_out, b_in0 = after(query_out, b_in0)
+    some_parts = [(queries,), (query_pair,), (query_out, query_mid)]
+    attended = attended_transposed(place, some_parts, stored_keys, stored_values, 0, 2)
+
+    (a_out, a_mid1), attended = after((a_out, a_mid1), attended)
+    own_a = plus(a_own, a_in[half:], a_mid1, a_out)
+    pair_a = paired(own_a)
+    mid_a = across(own_a)
+    b_mid0, own_a = after(b_mid0, own_a)
+    b_out = outward(plus(b_near[half:], b_mid0))
+    b_in, b_mid0 = after(b_in, b_mid0)
+    b_mid1 = across(plus(b_near[:half], b_in[:half]))
+
+    query_parts = some_parts + [(query_last, query_far)]
+    attended = attended_transposed(place, query_parts, stored_keys, stored_values, 2, 1, [attended])
+    (pair_a, mid_a), attended = after((pair_a, mid_a), attended)
+    far_a = across(pair_a)
+    out_a = outward(mid_a)
+    (attended, upstream_all), (pair_a, mid_a) = after((attended, upstream_all), (pair_a, mid_a))
+    grad_output = output_gradient(attended, upstream_all)
+    (b_out, b_mid1), grad_output = after((b_out, b_mid1), grad_output)
+    own_b = plus(b_own, b_in[half:], b_mid1, b_out)
+    pair_b = paired(own_b)
+    mid_b = across(own_b)
+    results = backward(0, [(own_a,), (own_b,)], None)
+    (far_a, out_a), results = after((far_a, out_a), results)
+    last_a = outward(far_a)
+
+    pair_b, mid_b, results = lax.optimization_barrier((pair_b, mid_b, results))
+    far_b = across(pair_b)
+    out_b = outward(mid_b)
+    results = backward(1, [(pair_a,), (pair_b,)], results)
+
+    far_b, out_b, results = lax.optimization_barrier((far_b, out_b, results))
+    last_b = outward(far_b)
+    results = backward(2, [(out_a, mid_a), (out_b, mid_b)], results)
+    (last_a, last_b), results = after((last_a, last_b), results)
+    query_grad, key_grad, value_grad = backward(3, [(last_a, far_a), (last_b, far_b)], results)
+
+    weights = (query_grad, key_grad, value_grad, query_weight, key_matrix, value_matrix)
+    to_sub, to_col = input_gradients(0, place, rows, *weights)
+    to_col = to_col + swap(to_sub, "sub")
+    from_col = swap(to_col, "col")
+    weights, to_col = after(weights, to_col)
+    to_sub, kept = input_gradients(1, place, rows, *weights)
+    from_sub = swap(to_sub, "sub")
+    normed_all, kept = after(normed_all, kept)
+    grad_query, grad_key, grad_value = weight_gradients(normed_all, query_grad, key_grad, value_grad, block=512)
+    from_col, _ = after(from_col, grad_query)
+    from_sub, from_col = after(from_sub, from_col)
+    grad_normed = plus(kept, from_sub, from_col)
+    return (grad_normed, grad_query, grad_key, grad_value, grad_output)
+
+
 def solution(mesh):
     in_specs = (
         P(("groups", "col", "sub"), "row"),
@@ -154,4 +611,5 @@
         P(("groups", "row"), ("col", "sub")),
         P(("groups", "col", "sub"), "row"),
     )
-    return jax.shard_map(shards, mesh=mesh, in_specs=in_specs, out_specs=out_specs, check_vma=False)
+    small = tuple(mesh.shape[axis] for axis in ("row", "col", "sub")) == (4, 2, 2)
+    return jax.shard_map(shards if small else general_shards, mesh=mesh, in_specs=in_specs, out_specs=out_specs, check_vma=False)

time: 384 us -> 209 us (0.54)
  waiting for transfers between devices: 204 us -> 30.3 us
  matrix products: 102 us -> 0 us
  Pallas kernels: 0 us -> 87.1 us
  starting transfers between devices: 0.19 us -> 55 us
  local copies, waits for them, and re-layouts: 59.2 us -> 7.12 us
  other arithmetic: 2.76 us -> 13.3 us
    psum x1 -> x0, waiting for transfers between devices: 122 us -> none  [shards(): attended_gradient = lax.psum(partial_sum.astype(jnp.bfloat16), 'row')]
    dot_general x23 -> x0, matrix products: 91.2 us -> none  [the longest x3 12 us: attend(): jnp.einsum('agqk,qagd->kad', soft_bf, gradient_heads, preferred_element_t...]
    pallas_call x0 -> x12, Pallas kernels: none -> 87.1 us  [the longest x4 23.7 us: attention_backward(): pl.pallas_call(functools.partial(backward_kernel, slot, quarter // HEAD_S...]
    all_gather x3 -> x2, waiting for transfers between devices: 80 us -> 0.02 us  [the longest x1 0.02 us: shards(): lax.all_gather(late_upstream, ('col', 'sub'), axis=0, tiled=True)]
    ppermute x0 -> x31, starting transfers between devices: none -> 54.9 us  [the longest x3 17.9 us: paired(): return lax.ppermute(x, 'row', [(0, 1), (1, 0), (2, 3), (3, 2)])]
    ppermute x0 -> x31, waiting for transfers between devices: none -> 30.3 us  [the longest x8 10.9 us: outward(): return lax.ppermute(x, 'row', [(1, 0), (2, 3)])]
    dynamic_update_slice x18 -> x0, local copies, waits for them, and re-layouts: 18.8 us -> none  [shards(): lax.map(per_sequence, (query_token_rows.reshape(sequence_list, SEQUENCE_L...]
    dynamic_slice x21 -> x0, local copies, waits for them, and re-layouts: 16.4 us -> none  [shards(): lax.map(per_sequence, (query_token_rows.reshape(sequence_list, SEQUENCE_L...]
  transfers between devices with their start and end apart: 5 -> 33, of which waited for: 3 -> 10; matrix products, arithmetic and copies ran while one was open for 42% -> 5% of each run, Pallas kernels for 0% -> 42%
where the time goes in v2:
time: 209 us; the launch traced here: 208 us
  Pallas kernels  87.1 us (42%)
  starting transfers between devices  55 us (26%)
  waiting for transfers between devices  30.3 us (14%)
  between operations  14.7 us (7%)
  other arithmetic  13.3 us (6%)
  local copies, waits for them, and re-layouts  7.12 us (3%)
    pallas_call x4, Pallas kernels, attention_backward(): pl.pallas_call(functools.partial(backward_kernel, slot, quarter // HEAD_S...  23.7 us
    ppermute x3, starting transfers between devices, paired(): return lax.ppermute(x, 'row', [(0, 1), (1, 0), (2, 3), (3, 2)])  17.9 us
    pallas_call x2, Pallas kernels, partial_products(): pl.pallas_call(partial_kernel, grid_spec=spec, out_shape=[jax.ShapeDtypeS...  17.7 us
    ppermute x4, starting transfers between devices, inward(): return lax.ppermute(x, 'row', [(0, 1), (3, 2)])  13 us
    pallas_call x1, Pallas kernels, weight_gradients(): pl.pallas_call(weights_kernel, grid=(feats // block,), in_specs=[pl.Block...  12.7 us
    pallas_call x2, Pallas kernels, attended_transposed(): pl.pallas_call(functools.partial(forward_kernel, [len(part) for part in p...  12.3 us
    pallas_call x2, Pallas kernels, input_gradients(): pl.pallas_call(functools.partial(input_kernel, half), grid_spec=spec, out...  12 us
    ppermute x8, waiting for transfers between devices, outward(): return lax.ppermute(x, 'row', [(1, 0), (2, 3)])  10.9 us
  transfers between devices with their start and end apart: 33, of which 10 were waited for; matrix products, arithmetic and copies ran while one was open for 5% of the time, Pallas kernels for 42%

profile of v2, /device:TPU:0, one launch (start us, length us, event | category | flops | bytes accessed | tf_op | source)
XLA Modules:
  0.0 207.6 jit_solution(137304749075025371)
XLA Ops:
  8.4 5.4 %collective-permute-start.1 = (bf16[192,2048]{1,0:T(8,128)(2,1)}, bf16[192,2048]{1,0:T(8,128)(2,1)S(1)}, u32[]{:S(2)}, u32[]{:S(2)}) collective-permute-start(bf16[192,2048]{1,0:T(8,128)(2,1)} %rest_0_.7), channel_id=1, source_target_pairs={{0,4},{4,0},{8,12},{12,8},{1,5},{5,1},{9,13},{13,9},{2,6},{6,2},{1... | collective-permute-start | bytes 2359304 | tf_op jit(solution)/shard_map/ppermute | solution.py:460
  13.9 1.5 collective-permute-start
  17.6 8.9 %gradient_partial.2 = (bf16[384,512]{1,0:T(8,128)(2,1)}, bf16[768,512]{1,0:T(8,128)(2,1)}, bf16[384,512]{1,0:T(8,128)(2,1)}) custom-call(s32[28]{0:T(128)} %compare_select_fusion.8.place_ref, bf16[192,2048]{1,0:T(8,128)(2,1)} %first_ref.1, bf16[192,2048]{1,0:T(8,128)(2,1)} %copy-done.31, bf16[2048,2048]{1,0:T(8,128)(2,1)} %weight_ref.3), custom_call_target="tpu_custom_call" | custom-call | flops 1048576 | bytes 65536 | tf_op jit(solution)/shard_map/gradient_partial/pallas_call | solution.py:237
  26.5 5.5 %collective-permute-done.1.refs_1_.rest_1_ = bf16[192,2048]{1,0:T(8,128)(2,1)S(1)} collective-permute-done((bf16[192,2048]{1,0:T(8,128)(2,1)}, bf16[192,2048]{1,0:T(8,128)(2,1)S(1)}, u32[]{:S(2)}, u32[]{:S(2)}) %collective-permute-start.1) | collective-permute-done | bytes 786464 | tf_op jit(solution)/shard_map/ppermute | solution.py:460
  33.6 3.2 %collective-permute-start.4 = (bf16[384,512]{1,0:T(8,128)(2,1)}, bf16[384,512]{1,0:T(8,128)(2,1)}, u32[]{:S(2)}, u32[]{:S(2)}) collective-permute-start(bf16[384,512]{1,0:T(8,128)(2,1)} %get-tuple-element.105), channel_id=1, source_target_pairs={{0,4},{12,8},{1,5},{13,9},{2,6},{14,10},{3,7},{15,11},{16,20},{28,... | collective-permute-start | bytes 1179656 | tf_op jit(solution)/shard_map/ppermute | solution.py:448
  36.8 1.6 collective-permute-start.8
  39.7 5.6 %collective-permute-start.10 = (bf16[768,512]{1,0:T(8,128)(2,1)}, bf16[768,512]{1,0:T(8,128)(2,1)}, u32[]{:S(2)}, u32[]{:S(2)}) collective-permute-start(bf16[768,512]{1,0:T(8,128)(2,1)} %get-tuple-element.111), channel_id=1, source_target_pairs={{0,4},{12,8},{1,5},{13,9},{2,6},{14,10},{3,7},{15,11},{16,20},{28,... | collective-permute-start | bytes 2359304 | tf_op jit(solution)/shard_map/ppermute | solution.py:448
  45.2 8.9 %gradient_partial.3 = (bf16[384,512]{1,0:T(8,128)(2,1)}, bf16[768,512]{1,0:T(8,128)(2,1)}, bf16[384,512]{1,0:T(8,128)(2,1)}) custom-call(s32[28]{0:T(128)} %compare_select_fusion.8.place_ref, bf16[192,2048]{1,0:T(8,128)(2,1)} %copy-done.30, bf16[192,2048]{1,0:T(8,128)(2,1)} %collective-permute-done.5.second_ref, bf16[2048,2048]{1,0:T(8,128)(2,1)} %weight_ref.3), custom_call_target="tpu_custom_call" | custom-call | flops 1048576 | bytes 65536 | tf_op jit(solution)/shard_map/gradient_partial/pallas_call | solution.py:237
  54.1 1.9 add_convert_fusion.8
  56.8 2.8 %collective-permute-start.9 = (bf16[384,512]{1,0:T(8,128)(2,1)}, bf16[384,512]{1,0:T(8,128)(2,1)}, u32[]{:S(2)}, u32[]{:S(2)}) collective-permute-start(bf16[384,512]{1,0:T(8,128)(2,1)} %get-tuple-element.126), channel_id=1, source_target_pairs={{0,4},{12,8},{1,5},{13,9},{2,6},{14,10},{3,7},{15,11},{16,20},{28,... | collective-permute-start | bytes 1179656 | tf_op jit(solution)/shard_map/ppermute | solution.py:448
  61.1 1.5 collective-permute-done.10
  66.1 5.0 %collective-permute-done.9 = bf16[384,512]{1,0:T(8,128)(2,1)} collective-permute-done((bf16[384,512]{1,0:T(8,128)(2,1)}, bf16[384,512]{1,0:T(8,128)(2,1)}, u32[]{:S(2)}, u32[]{:S(2)}) %collective-permute-start.9) | collective-permute-done | bytes 393248 | tf_op jit(solution)/shard_map/ppermute | solution.py:448
  77.6 7.3 %attention_forward.2.refs_8_ = bf16[2048,768]{1,0:T(8,128)(2,1)S(1)} custom-call(s32[28]{0:T(128)S(1)} %copy-done.29, bf16[192,2048]{1,0:T(8,128)(2,1)S(1)} %copy-done.3, bf16[192,2048]{1,0:T(8,128)(2,1)S(1)} %copy-done.10, bf16[192,2048]{1,0:T(8,128)(2,1)S(1)} %copy-done.13, bf16[192,2048]{1,0:T(8,128)(2,1)S(1)} %copy-done.7, ...), custom_call_target="tpu_custom_call" | custom-call | flops 1048576 | bytes 65536 | tf_op jit(solution)/shard_map/attention_forward/pallas_call | solution.py:107
  87.8 6.3 %collective-permute-start.14 = (bf16[384,512]{1,0:T(8,128)(2,1)S(1)}, bf16[384,512]{1,0:T(8,128)(2,1)}, u32[]{:S(2)}, u32[]{:S(2)}) collective-permute-start(bf16[384,512]{1,0:T(8,128)(2,1)S(1)} %add_convert_fusion.5.rest_6_), channel_id=1, source_target_pairs={{0,4},{4,0},{8,12},{12,8},{1,5},{5,1},{9,13},{13,9},{2,6},{6,2},{1... | collective-permute-start | bytes 1179656 | tf_op jit(solution)/shard_map/ppermute | solution.py:460
  97.9 1.6 collective-permute-done.11.refs_4_.rest_4_
  99.5 5.0 %attention_forward.3.attended_ref = bf16[2048,768]{1,0:T(8,128)(2,1)S(1)} custom-call(s32[28]{0:T(128)S(1)} %copy-done.29, bf16[192,2048]{1,0:T(8,128)(2,1)S(1)} %copy-done.4, bf16[192,2048]{1,0:T(8,128)(2,1)S(1)} %copy-done.10, bf16[192,2048]{1,0:T(8,128)(2,1)S(1)} %copy-done.14, bf16[192,2048]{1,0:T(8,128)(2,1)S(1)} %copy-done.7, ...), custom_call_target="tpu_custom_call", output_to_operand_aliasing={{}: (9, {})} | custom-call | flops 1048576 | bytes 65536 | tf_op jit(solution)/shard_map/attention_forward/pallas_call | solution.py:107
  104.6 3.5 %collective-permute-done.14.rest_6_ = bf16[384,512]{1,0:T(8,128)(2,1)} collective-permute-done((bf16[384,512]{1,0:T(8,128)(2,1)S(1)}, bf16[384,512]{1,0:T(8,128)(2,1)}, u32[]{:S(2)}, u32[]{:S(2)}) %collective-permute-start.14) | collective-permute-done | bytes 393248 | tf_op jit(solution)/shard_map/ppermute | solution.py:460
  110.8 1.9 copy-done.24
  112.7 8.6 %output_gradient.1 = bf16[2048,2048]{1,0:T(8,128)(2,1)} custom-call(bf16[2048,768]{1,0:T(8,128)(2,1)S(1)} %attention_forward.3.attended_ref, bf16[768,2048]{1,0:T(8,128)(2,1)S(1)} %copy-done.24), custom_call_target="tpu_custom_call" | custom-call | flops 1048576 | bytes 65536 | tf_op jit(solution)/shard_map/output_gradient/pallas_call | solution.py:254
  123.4 6.2 %collective-permute-start.23 = (bf16[384,512]{1,0:T(8,128)(2,1)S(1)}, bf16[384,512]{1,0:T(8,128)(2,1)S(1)}, u32[]{:S(2)}, u32[]{:S(2)}) collective-permute-start(bf16[384,512]{1,0:T(8,128)(2,1)S(1)} %add_convert_fusion.1.rest_7_), channel_id=1, source_target_pairs={{0,4},{4,0},{8,12},{12,8},{1,5},{5,1},{9,13},{13,9},{2,6},{6,2},{1... | collective-permute-start | bytes 1179656 | tf_op jit(solution)/shard_map/ppermute | solution.py:460
  129.6 5.5 %attention_backward.4 = (bf16[768,2048]{1,0:T(8,128)(2,1)S(1)}, f32[768,256]{1,0:T(8,128)S(1)}, f32[768,256]{1,0:T(8,128)S(1)}) custom-call(s32[28]{0:T(128)S(1)} %copy-done.29, bf16[768,256]{1,0:T(8,128)(2,1)S(1)} %copy-done.18, bf16[768,256]{1,0:T(8,128)(2,1)S(1)} %copy-done.21, bf16[192,2048]{1,0:T(8,128)(2,1)S(1)} %copy-done.5, ...), custom_call_target="tpu_custom_call" | custom-call | flops 1048576 | bytes 65536 | tf_op jit(solution)/shard_map/attention_backward/pallas_call | solution.py:188
  138.7 5.8 %attention_backward.5 = (bf16[768,2048]{1,0:T(8,128)(2,1)S(1)}, f32[768,256]{1,0:T(8,128)S(1)}, f32[768,256]{1,0:T(8,128)S(1)}) custom-call(s32[28]{0:T(128)S(1)} %copy-done.29, bf16[768,256]{1,0:T(8,128)(2,1)S(1)} %copy-done.18, bf16[768,256]{1,0:T(8,128)(2,1)S(1)} %copy-done.21, ...), custom_call_target="tpu_custom_call", output_to_operand_aliasing={{0}: (11, {}), {1}: (12, {}), {2}: (13, {})} | custom-call | flops 1048576 | bytes 65536 | tf_op jit(solution)/shard_map/attention_backward/pallas_call | solution.py:188
  144.5 6.5 %collective-permute-done.26.rest_8_ = bf16[384,512]{1,0:T(8,128)(2,1)S(1)} collective-permute-done((bf16[384,512]{1,0:T(8,128)(2,1)S(1)}, bf16[384,512]{1,0:T(8,128)(2,1)S(1)}, u32[]{:S(2)}, u32[]{:S(2)}) %collective-permute-start.26) | collective-permute-done | bytes 393248 | tf_op jit(solution)/shard_map/ppermute | solution.py:456
  152.3 6.2 %attention_backward.6 = (bf16[768,2048]{1,0:T(8,128)(2,1)S(1)}, f32[768,256]{1,0:T(8,128)S(1)}, f32[768,256]{1,0:T(8,128)S(1)}) custom-call(s32[28]{0:T(128)S(1)} %copy-done.29, bf16[768,256]{1,0:T(8,128)(2,1)S(1)} %copy-done.18, bf16[768,256]{1,0:T(8,128)(2,1)S(1)} %copy-done.21, ...), custom_call_target="tpu_custom_call", output_to_operand_aliasing={{0}: (13, {}), {1}: (14, {}), {2}: (15, {})} | custom-call | flops 1048576 | bytes 65536 | tf_op jit(solution)/shard_map/attention_backward/pallas_call | solution.py:188
  158.6 2.8 %collective-permute-done.27.rest_8_ = bf16[384,512]{1,0:T(8,128)(2,1)S(1)} collective-permute-done((bf16[384,512]{1,0:T(8,128)(2,1)S(1)}, bf16[384,512]{1,0:T(8,128)(2,1)S(1)}, u32[]{:S(2)}, u32[]{:S(2)}) %collective-permute-start.27) | collective-permute-done | bytes 393248 | tf_op jit(solution)/shard_map/ppermute | solution.py:456
  161.4 6.2 %attention_backward.7 = (bf16[768,2048]{1,0:T(8,128)(2,1)S(1)}, f32[768,256]{1,0:T(8,128)S(1)}, f32[768,256]{1,0:T(8,128)S(1)}) custom-call(s32[28]{0:T(128)S(1)} %copy-done.29, bf16[768,256]{1,0:T(8,128)(2,1)S(1)} %copy-done.18, bf16[768,256]{1,0:T(8,128)(2,1)S(1)} %copy-done.21, ...), custom_call_target="tpu_custom_call", output_to_operand_aliasing={{0}: (13, {}), {1}: (14, {}), {2}: (15, {})} | custom-call | flops 1048576 | bytes 65536 | tf_op jit(solution)/shard_map/attention_backward/pallas_call | solution.py:188
  167.7 5.7 %input_gradients.2 = (bf16[192,2048]{1,0:T(8,128)(2,1)S(1)}, bf16[192,2048]{1,0:T(8,128)(2,1)S(1)}) custom-call(s32[28]{0:T(128)S(1)} %copy-done.29, bf16[768,2048]{1,0:T(8,128)(2,1)S(1)} %get-tuple-element.174.dq_ref, f32[768,256]{1,0:T(8,128)S(1)} %get-tuple-element.175.dk_ref, f32[768,256]{1,0:T(8,128)S(1)} %get-tuple-element.176.dv_ref, ...), custom_call_target="tpu_custom_call" | custom-call | flops 1048576 | bytes 65536 | tf_op jit(solution)/shard_map/input_gradients/pallas_call | solution.py:308
  173.4 2.3 %collective-permute-done.28 = bf16[192,2048]{1,0:T(8,128)(2,1)S(1)} collective-permute-done((bf16[192,2048]{1,0:T(8,128)(2,1)S(1)}, bf16[192,2048]{1,0:T(8,128)(2,1)S(1)}, u32[]{:S(2)}, u32[]{:S(2)}) %collective-permute-start.28) | collective-permute-done | bytes 786464 | tf_op jit(solution)/shard_map/ppermute | solution.py:444
  176.9 1.5 collective-permute-start.30
  178.4 6.3 %input_gradients.3 = (bf16[192,2048]{1,0:T(8,128)(2,1)}, bf16[192,2048]{1,0:T(8,128)(2,1)S(1)}) custom-call(s32[28]{0:T(128)S(1)} %copy-done.29, bf16[768,2048]{1,0:T(8,128)(2,1)S(1)} %get-tuple-element.174.dq_ref, f32[768,256]{1,0:T(8,128)S(1)} %get-tuple-element.175.dk_ref, f32[768,256]{1,0:T(8,128)S(1)} %get-tuple-element.176.dv_ref, ...), custom_call_target="tpu_custom_call" | custom-call | flops 1048576 | bytes 65536 | tf_op jit(solution)/shard_map/input_gradients/pallas_call | solution.py:308
  185.6 12.7 %weight_gradients.1 = (bf16[2048,2048]{1,0:T(8,128)(2,1)}, bf16[2048,256]{1,0:T(8,128)(2,1)}, bf16[2048,256]{1,0:T(8,128)(2,1)}) custom-call(bf16[768,2048]{1,0:T(8,128)(2,1)} %all-gather.3.cloned.1.call-done.n_ref, bf16[768,2048]{1,0:T(8,128)(2,1)} %copy-done, f32[768,256]{1,0:T(8,128)} %copy-done.1, f32[768,256]{1,0:T(8,128)} %copy-done.2), custom_call_target="tpu_custom_call" | custom-call | flops 1048576 | bytes 65536 | tf_op jit(solution)/shard_map/weight_gradients/pallas_call | solution.py:276
  198.4 2.4 %add_convert_fusion = bf16[192,2048]{1,0:T(8,128)(2,1)} fusion(bf16[192,2048]{1,0:T(8,128)(2,1)} %collective-permute-done.30, bf16[192,2048]{1,0:T(8,128)(2,1)S(1)} %collective-permute-done.29, bf16[192,2048]{1,0:T(8,128)(2,1)S(1)} %copy-done.28), kind=kLoop, calls=%fused_computation | loop fusion | flops 2359296 | bytes 3145728 | tf_op jit(solution)/shard_map/convert_element_type | solution.py:468
  (142 shorter events, 37.0 us)
Async XLA Ops:
  7.2 103.6 %all-gather.5.cloned.1.call-start = ((), (), s32[]{:S(2)}) async-start(), calls=%async_computation.1 | async-start | bytes 3932160 | tf_op jit(solution)/shard_map/all_gather | solution.py:525
  7.2 9.5 %collective-permute-start.3 = (bf16[192,2048]{1,0:T(8,128)(2,1)}, bf16[192,2048]{1,0:T(8,128)(2,1)S(1)}, u32[]{:S(2)}, u32[]{:S(2)}) collective-permute-start(bf16[192,2048]{1,0:T(8,128)(2,1)} %first_ref.1), channel_id=1, source_target_pairs={{0,1},{1,0},{2,3},{3,2},{4,5},{5,4},{6,7},{7,6},{8,9},{9,8},{10,11... | collective-permute-start | bytes 2359304 | tf_op jit(solution)/shard_map/ppermute | solution.py:444
  7.7 18.7 %collective-permute-start.2 = (bf16[192,2048]{1,0:T(8,128)(2,1)}, bf16[192,2048]{1,0:T(8,128)(2,1)S(1)}, u32[]{:S(2)}, u32[]{:S(2)}) collective-permute-start(bf16[192,2048]{1,0:T(8,128)(2,1)} %rest_0_.7), channel_id=1, source_target_pairs={{4,8},{8,4},{5,9},{9,5},{6,10},{10,6},{7,11},{11,7},{20,24},{24,20... | collective-permute-start | bytes 2359304 | tf_op jit(solution)/shard_map/ppermute | solution.py:452
  8.4 23.6 %collective-permute-start.1 = (bf16[192,2048]{1,0:T(8,128)(2,1)}, bf16[192,2048]{1,0:T(8,128)(2,1)S(1)}, u32[]{:S(2)}, u32[]{:S(2)}) collective-permute-start(bf16[192,2048]{1,0:T(8,128)(2,1)} %rest_0_.7), channel_id=1, source_target_pairs={{0,4},{4,0},{8,12},{12,8},{1,5},{5,1},{9,13},{13,9},{2,6},{6,2},{1... | collective-permute-start | bytes 2359304 | tf_op jit(solution)/shard_map/ppermute | solution.py:460
  13.9 19.6 %collective-permute-start = (bf16[192,2048]{1,0:T(8,128)(2,1)}, bf16[192,2048]{1,0:T(8,128)(2,1)S(1)}, u32[]{:S(2)}, u32[]{:S(2)}) collective-permute-start(bf16[192,2048]{1,0:T(8,128)(2,1)} %first_ref.1), channel_id=1, source_target_pairs={{0,2},{2,0},{1,3},{3,1},{4,6},{6,4},{5,7},{7,5},{8,10},{10,8},{9,1... | collective-permute-start | bytes 2359304 | tf_op jit(solution)/shard_map/ppermute | solution.py:444
  33.5 152.1 %all-gather.3.cloned.1.call-start = ((), (), s32[]{:S(2)}) async-start(), calls=%async_computation | async-start | bytes 3932160 | tf_op jit(solution)/shard_map/all_gather | solution.py:526
  33.5 11.7 %collective-permute-start.5 = (bf16[192,2048]{1,0:T(8,128)(2,1)S(1)}, bf16[192,2048]{1,0:T(8,128)(2,1)}, u32[]{:S(2)}, u32[]{:S(2)}) collective-permute-start(bf16[192,2048]{1,0:T(8,128)(2,1)S(1)} %collective-permute-done.first_ref), channel_id=1, source_target_pairs={{0,1},{1,0},{2,3},{3,2},{4,5},{5,4},{6,7},{7,6},{8,9},{9,8},{10,11... | collective-permute-start | bytes 2359304 | tf_op jit(solution)/shard_map/ppermute | solution.py:444
  33.6 20.5 %collective-permute-start.4 = (bf16[384,512]{1,0:T(8,128)(2,1)}, bf16[384,512]{1,0:T(8,128)(2,1)}, u32[]{:S(2)}, u32[]{:S(2)}) collective-permute-start(bf16[384,512]{1,0:T(8,128)(2,1)} %get-tuple-element.105), channel_id=1, source_target_pairs={{0,4},{12,8},{1,5},{13,9},{2,6},{14,10},{3,7},{15,11},{16,20},{28,... | collective-permute-start | bytes 1179656 | tf_op jit(solution)/shard_map/ppermute | solution.py:448
  36.8 22.8 %collective-permute-start.8 = (bf16[192,2048]{1,0:T(8,128)(2,1)S(1)}, bf16[192,2048]{1,0:T(8,128)(2,1)}, u32[]{:S(2)}, u32[]{:S(2)}) collective-permute-start(bf16[192,2048]{1,0:T(8,128)(2,1)S(1)} %collective-permute-done.1.refs_1_.rest_1_), channel_id=1, source_target_pairs={{4,8},{8,4},{5,9},{9,5},{6,10},{10,6},{7,11},{11,7},{20,24},{24,20... | collective-permute-start | bytes 2359304 | tf_op jit(solution)/shard_map/ppermute | solution.py:452
  38.4 22.7 %collective-permute-start.7 = (bf16[192,2048]{1,0:T(8,128)(2,1)S(1)}, bf16[192,2048]{1,0:T(8,128)(2,1)S(1)}, u32[]{:S(2)}, u32[]{:S(2)}) collective-permute-start(bf16[192,2048]{1,0:T(8,128)(2,1)S(1)} %collective-permute-done.2.refs_3_.rest_3_), channel_id=1, source_target_pairs={{4,0},{8,12},{5,1},{9,13},{6,2},{10,14},{7,3},{11,15},{20,16},{24,... | collective-permute-start | bytes 2359304 | tf_op jit(solution)/shard_map/ppermute | solution.py:456
  39.7 23.0 %collective-permute-start.10 = (bf16[768,512]{1,0:T(8,128)(2,1)}, bf16[768,512]{1,0:T(8,128)(2,1)}, u32[]{:S(2)}, u32[]{:S(2)}) collective-permute-start(bf16[768,512]{1,0:T(8,128)(2,1)} %get-tuple-element.111), channel_id=1, source_target_pairs={{0,4},{12,8},{1,5},{13,9},{2,6},{14,10},{3,7},{15,11},{16,20},{28,... | collective-permute-start | bytes 2359304 | tf_op jit(solution)/shard_map/ppermute | solution.py:448
  56.1 5.0 %collective-permute-start.6 = (bf16[384,512]{1,0:T(8,128)(2,1)}, bf16[384,512]{1,0:T(8,128)(2,1)S(1)}, u32[]{:S(2)}, u32[]{:S(2)}) collective-permute-start(bf16[384,512]{1,0:T(8,128)(2,1)} %add_convert_fusion.8), channel_id=1, source_target_pairs={{4,8},{8,4},{5,9},{9,5},{6,10},{10,6},{7,11},{11,7},{20,24},{24,20... | collective-permute-start | bytes 1179656 | tf_op jit(solution)/shard_map/ppermute | solution.py:452
  56.8 14.3 %collective-permute-start.9 = (bf16[384,512]{1,0:T(8,128)(2,1)}, bf16[384,512]{1,0:T(8,128)(2,1)}, u32[]{:S(2)}, u32[]{:S(2)}) collective-permute-start(bf16[384,512]{1,0:T(8,128)(2,1)} %get-tuple-element.126), channel_id=1, source_target_pairs={{0,4},{12,8},{1,5},{13,9},{2,6},{14,10},{3,7},{15,11},{16,20},{28,... | collective-permute-start | bytes 1179656 | tf_op jit(solution)/shard_map/ppermute | solution.py:448
  59.6 34.4 %collective-permute-start.19 = (bf16[768,512]{1,0:T(8,128)(2,1)}, bf16[768,512]{1,0:T(8,128)(2,1)S(1)}, u32[]{:S(2)}, u32[]{:S(2)}) collective-permute-start(bf16[768,512]{1,0:T(8,128)(2,1)} %get-tuple-element.129), channel_id=1, source_target_pairs={{0,4},{12,8},{1,5},{13,9},{2,6},{14,10},{3,7},{15,11},{16,20},{28,... | collective-permute-start | bytes 2359304 | tf_op jit(solution)/shard_map/ppermute | solution.py:448
  64.1 20.9 %collective-permute-start.13 = (bf16[384,512]{1,0:T(8,128)(2,1)S(1)}, bf16[384,512]{1,0:T(8,128)(2,1)S(1)}, u32[]{:S(2)}, u32[]{:S(2)}) collective-permute-start(bf16[384,512]{1,0:T(8,128)(2,1)S(1)} %get-tuple-element.193), channel_id=1, source_target_pairs={{4,8},{8,4},{5,9},{9,5},{6,10},{10,6},{7,11},{11,7},{20,24},{24,20... | collective-permute-start | bytes 1179656 | tf_op jit(solution)/shard_map/ppermute | solution.py:452
  64.8 20.2 %collective-permute-start.12 = (bf16[384,512]{1,0:T(8,128)(2,1)S(1)}, bf16[384,512]{1,0:T(8,128)(2,1)S(1)}, u32[]{:S(2)}, u32[]{:S(2)}) collective-permute-start(bf16[384,512]{1,0:T(8,128)(2,1)S(1)} %get-tuple-element.194), channel_id=1, source_target_pairs={{4,0},{8,12},{5,1},{9,13},{6,2},{10,14},{7,3},{11,15},{20,16},{24,... | collective-permute-start | bytes 1179656 | tf_op jit(solution)/shard_map/ppermute | solution.py:456
  72.3 21.8 %collective-permute-start.18 = (bf16[384,512]{1,0:T(8,128)(2,1)S(1)}, bf16[384,512]{1,0:T(8,128)(2,1)S(1)}, u32[]{:S(2)}, u32[]{:S(2)}) collective-permute-start(bf16[384,512]{1,0:T(8,128)(2,1)S(1)} %add_convert_fusion.4), channel_id=1, source_target_pairs={{4,8},{8,4},{5,9},{9,5},{6,10},{10,6},{7,11},{11,7},{20,24},{24,20... | collective-permute-start | bytes 1179656 | tf_op jit(solution)/shard_map/ppermute | solution.py:452
  73.0 26.5 %collective-permute-start.11 = (bf16[192,2048]{1,0:T(8,128)(2,1)}, bf16[192,2048]{1,0:T(8,128)(2,1)S(1)}, u32[]{:S(2)}, u32[]{:S(2)}) collective-permute-start(bf16[192,2048]{1,0:T(8,128)(2,1)} %collective-permute-done.8.refs_5_.rest_5_), channel_id=1, source_target_pairs={{4,0},{8,12},{5,1},{9,13},{6,2},{10,14},{7,3},{11,15},{20,16},{24,... | collective-permute-start | bytes 2359304 | tf_op jit(solution)/shard_map/ppermute | solution.py:456
  86.3 18.2 %collective-permute-start.15 = (bf16[384,512]{1,0:T(8,128)(2,1)S(1)}, bf16[384,512]{1,0:T(8,128)(2,1)}, u32[]{:S(2)}, u32[]{:S(2)}) collective-permute-start(bf16[384,512]{1,0:T(8,128)(2,1)S(1)} %add_convert_fusion.5.rest_6_), channel_id=1, source_target_pairs={{4,8},{8,4},{5,9},{9,5},{6,10},{10,6},{7,11},{11,7},{20,24},{24,20... | collective-permute-start | bytes 1179656 | tf_op jit(solution)/shard_map/ppermute | solution.py:452
  87.8 20.3 %collective-permute-start.14 = (bf16[384,512]{1,0:T(8,128)(2,1)S(1)}, bf16[384,512]{1,0:T(8,128)(2,1)}, u32[]{:S(2)}, u32[]{:S(2)}) collective-permute-start(bf16[384,512]{1,0:T(8,128)(2,1)S(1)} %add_convert_fusion.5.rest_6_), channel_id=1, source_target_pairs={{0,4},{4,0},{8,12},{12,8},{1,5},{5,1},{9,13},{13,9},{2,6},{6,2},{1... | collective-permute-start | bytes 1179656 | tf_op jit(solution)/shard_map/ppermute | solution.py:460
  95.2 26.1 %collective-permute-start.21 = (bf16[384,512]{1,0:T(8,128)(2,1)}, bf16[384,512]{1,0:T(8,128)(2,1)}, u32[]{:S(2)}, u32[]{:S(2)}) collective-permute-start(bf16[384,512]{1,0:T(8,128)(2,1)} %get-tuple-element.191), channel_id=1, source_target_pairs={{4,8},{8,4},{5,9},{9,5},{6,10},{10,6},{7,11},{11,7},{20,24},{24,20... | collective-permute-start | bytes 1179656 | tf_op jit(solution)/shard_map/ppermute | solution.py:452
  96.6 24.7 %collective-permute-start.20 = (bf16[384,512]{1,0:T(8,128)(2,1)}, bf16[384,512]{1,0:T(8,128)(2,1)}, u32[]{:S(2)}, u32[]{:S(2)}) collective-permute-start(bf16[384,512]{1,0:T(8,128)(2,1)} %get-tuple-element.192), channel_id=1, source_target_pairs={{4,0},{8,12},{5,1},{9,13},{6,2},{10,14},{7,3},{11,15},{20,16},{24,... | collective-permute-start | bytes 1179656 | tf_op jit(solution)/shard_map/ppermute | solution.py:456
  108.0 27.1 %collective-permute-start.16 = (bf16[384,512]{1,0:T(8,128)(2,1)}, bf16[384,512]{1,0:T(8,128)(2,1)}, u32[]{:S(2)}, u32[]{:S(2)}) collective-permute-start(bf16[384,512]{1,0:T(8,128)(2,1)} %collective-permute-done.14.rest_6_), channel_id=1, source_target_pairs={{4,8},{8,4},{5,9},{9,5},{6,10},{10,6},{7,11},{11,7},{20,24},{24,20... | collective-permute-start | bytes 1179656 | tf_op jit(solution)/shard_map/ppermute | solution.py:452
  109.4 25.7 %collective-permute-start.17 = (bf16[384,512]{1,0:T(8,128)(2,1)}, bf16[384,512]{1,0:T(8,128)(2,1)}, u32[]{:S(2)}, u32[]{:S(2)}) collective-permute-start(bf16[384,512]{1,0:T(8,128)(2,1)} %collective-permute-done.15.rest_7_), channel_id=1, source_target_pairs={{4,0},{8,12},{5,1},{9,13},{6,2},{10,14},{7,3},{11,15},{20,16},{24,... | collective-permute-start | bytes 1179656 | tf_op jit(solution)/shard_map/ppermute | solution.py:456
  122.7 12.4 %collective-permute-start.24 = (bf16[384,512]{1,0:T(8,128)(2,1)S(1)}, bf16[384,512]{1,0:T(8,128)(2,1)S(1)}, u32[]{:S(2)}, u32[]{:S(2)}) collective-permute-start(bf16[384,512]{1,0:T(8,128)(2,1)S(1)} %add_convert_fusion.1.rest_7_), channel_id=1, source_target_pairs={{4,8},{8,4},{5,9},{9,5},{6,10},{10,6},{7,11},{11,7},{20,24},{24,20... | collective-permute-start | bytes 1179656 | tf_op jit(solution)/shard_map/ppermute | solution.py:452
  123.4 11.9 %collective-permute-start.23 = (bf16[384,512]{1,0:T(8,128)(2,1)S(1)}, bf16[384,512]{1,0:T(8,128)(2,1)S(1)}, u32[]{:S(2)}, u32[]{:S(2)}) collective-permute-start(bf16[384,512]{1,0:T(8,128)(2,1)S(1)} %add_convert_fusion.1.rest_7_), channel_id=1, source_target_pairs={{0,4},{4,0},{8,12},{12,8},{1,5},{5,1},{9,13},{13,9},{2,6},{6,2},{1... | collective-permute-start | bytes 1179656 | tf_op jit(solution)/shard_map/ppermute | solution.py:460
  135.3 9.3 %collective-permute-start.25 = (bf16[384,512]{1,0:T(8,128)(2,1)S(1)}, bf16[384,512]{1,0:T(8,128)(2,1)S(1)}, u32[]{:S(2)}, u32[]{:S(2)}) collective-permute-start(bf16[384,512]{1,0:T(8,128)(2,1)S(1)} %collective-permute-done.23.rest_7_), channel_id=1, source_target_pairs={{4,8},{8,4},{5,9},{9,5},{6,10},{10,6},{7,11},{11,7},{20,24},{24,20... | collective-permute-start | bytes 1179656 | tf_op jit(solution)/shard_map/ppermute | solution.py:452
  136.0 15.1 %collective-permute-start.26 = (bf16[384,512]{1,0:T(8,128)(2,1)S(1)}, bf16[384,512]{1,0:T(8,128)(2,1)S(1)}, u32[]{:S(2)}, u32[]{:S(2)}) collective-permute-start(bf16[384,512]{1,0:T(8,128)(2,1)S(1)} %collective-permute-done.24.rest_9_), channel_id=1, source_target_pairs={{4,0},{8,12},{5,1},{9,13},{6,2},{10,14},{7,3},{11,15},{20,16},{24,... | collective-permute-start | bytes 1179656 | tf_op jit(solution)/shard_map/ppermute | solution.py:456
  137.3 21.3 %collective-permute-start.22 = (bf16[384,512]{1,0:T(8,128)(2,1)}, bf16[384,512]{1,0:T(8,128)(2,1)S(1)}, u32[]{:S(2)}, u32[]{:S(2)}) collective-permute-start(bf16[384,512]{1,0:T(8,128)(2,1)} %collective-permute-done.16.rest_7_), channel_id=1, source_target_pairs={{4,0},{8,12},{5,1},{9,13},{6,2},{10,14},{7,3},{11,15},{20,16},{24,... | collective-permute-start | bytes 1179656 | tf_op jit(solution)/shard_map/ppermute | solution.py:456
  151.0 10.4 %collective-permute-start.27 = (bf16[384,512]{1,0:T(8,128)(2,1)S(1)}, bf16[384,512]{1,0:T(8,128)(2,1)S(1)}, u32[]{:S(2)}, u32[]{:S(2)}) collective-permute-start(bf16[384,512]{1,0:T(8,128)(2,1)S(1)} %collective-permute-done.25.rest_9_), channel_id=1, source_target_pairs={{4,0},{8,12},{5,1},{9,13},{6,2},{10,14},{7,3},{11,15},{20,16},{24,... | collective-permute-start | bytes 1179656 | tf_op jit(solution)/shard_map/ppermute | solution.py:456
  176.9 21.5 %collective-permute-start.30 = (bf16[192,2048]{1,0:T(8,128)(2,1)}, bf16[192,2048]{1,0:T(8,128)(2,1)}, u32[]{:S(2)}, u32[]{:S(2)}) collective-permute-start(bf16[192,2048]{1,0:T(8,128)(2,1)} %add.61), channel_id=1, source_target_pairs={{0,2},{2,0},{1,3},{3,1},{4,6},{6,4},{5,7},{7,5},{8,10},{10,8},{9,1... | collective-permute-start | bytes 2359304 | tf_op jit(solution)/shard_map/ppermute | solution.py:444
  185.6 12.7 %collective-permute-start.29 = (bf16[192,2048]{1,0:T(8,128)(2,1)}, bf16[192,2048]{1,0:T(8,128)(2,1)S(1)}, u32[]{:S(2)}, u32[]{:S(2)}) collective-permute-start(bf16[192,2048]{1,0:T(8,128)(2,1)} %get-tuple-element.182), channel_id=1, source_target_pairs={{0,1},{1,0},{2,3},{3,2},{4,5},{5,4},{6,7},{7,6},{8,9},{9,8},{10,11... | collective-permute-start | bytes 2359304 | tf_op jit(solution)/shard_map/ppermute | solution.py:444
  (42 other events, 512.3 us)
Sparse Core Ops, SparseCore 0:
  33.6 27.5 all-gather.4
  62.7 28.5 all-gather.2

commit v3 on v2

--- a/solution.py
+++ b/solution.py
@@ -21,6 +21,7 @@
 HEAD_ORDER = ((0, 1, 2, 3), (1, 0, 2, 3), (2, 3, 1, 0), (3, 2, 1, 0))
 BLOCK = 128
 GROUP = 4
+PAIR = 2
 COST = pl.CostEstimate(flops=1 << 20, bytes_accessed=1 << 16, transcendentals=0)
 STREAMED = pltpu.CompilerParams(vmem_limit_bytes=60 * 1024 * 1024)
 PARAMS = pltpu.CompilerParams(vmem_limit_bytes=24 * 1024 * 1024)
@@ -39,8 +40,8 @@
     return raised * (1.0 / total)
 
 
-def stack(ref, rows, heads):
-    return jnp.concatenate([ref[rows, h * HEAD_SIZE : (h + 1) * HEAD_SIZE] for h in range(heads)])
+def stack(ref, rows, first, last):
+    return jnp.concatenate([ref[rows, h * HEAD_SIZE : (h + 1) * HEAD_SIZE] for h in range(first, last)])
 
 
 def assemble(place_ref, refs, groups, whole_ref):
@@ -151,17 +152,19 @@
     for start in range(0, L, BLOCK):
         stop = start + BLOCK
         here = pl.ds(pl.multiple_of(s * L + start, BLOCK), BLOCK)
-        stacked = stack(q_ref, here, heads)
-        grads = stack(grad_ref, here, heads)
-        soft = probabilities(keys[:stop], stacked, start)
-        soft_grad = lax.dot_general(values[:stop], grads, CONTRACT_LAST, preferred_element_type=F32)
-        dots = jnp.sum(soft * soft_grad, axis=0, keepdims=True)
-        score_grad = (soft * (soft_grad - dots)).astype(BF)
-        dv_ref[:stop, :] += jnp.dot(soft.astype(BF), grads, preferred_element_type=F32)
-        dk_ref[:stop, :] += jnp.dot(score_grad, stacked, preferred_element_type=F32) * SCALE
-        dq_t = (jnp.dot(keys_t[:, :stop], score_grad, preferred_element_type=F32) * SCALE).astype(BF)
-        for h in range(heads):
-            dq_ref[start:stop, h * HEAD_SIZE : (h + 1) * HEAD_SIZE] = dq_t[:, h * BLOCK : (h + 1) * BLOCK].T
+        for first in range(0, heads, PAIR):
+            stacked = stack(q_ref, here, first, first + PAIR)
+            grads = stack(grad_ref, here, first, first + PAIR)
+            soft = probabilities(keys[:stop], stacked, start)
+            soft_grad = lax.dot_general(values[:stop], grads, CONTRACT_LAST, preferred_element_type=F32)
+            dots = jnp.sum(soft * soft_grad, axis=0, keepdims=True)
+            score_grad = (soft * (soft_grad - dots)).astype(BF)
+            dv_ref[:stop, :] += jnp.dot(soft.astype(BF), grads, preferred_element_type=F32)
+            dk_ref[:stop, :] += jnp.dot(score_grad, stacked, preferred_element_type=F32) * SCALE
+            dq_t = (jnp.dot(keys_t[:, :stop], score_grad, preferred_element_type=F32) * SCALE).astype(BF)
+            for n in range(PAIR):
+                h = first + n
+                dq_ref[start:stop, h * HEAD_SIZE : (h + 1) * HEAD_SIZE] = dq_t[:, n * BLOCK : (n + 1) * BLOCK].T
 
 
 def attention_backward(slot, place, parts, keys, values, chunks, earlier):

time: 209 us -> 211 us (level)
  Pallas kernels: 87.1 us -> 91.9 us
  waiting for transfers between devices: 30.3 us -> 27.5 us
    pallas_call x4, Pallas kernels: 23.7 us -> 28.5 us  [attention_backward(): pl.pallas_call(functools.partial(backward_kernel, slot, quarter // HEAD_S...]
    ppermute x8, waiting for transfers between devices: 10.9 us -> 8.18 us  [outward(): return lax.ppermute(x, 'row', [(1, 0), (2, 3)])]
  transfers between devices with their start and end apart: 33 -> 33, of which waited for: 10 -> 9; matrix products, arithmetic and copies ran while one was open for 5% -> 5% of each run, Pallas kernels for 42% -> 44%
where the time goes in v3:
time: 211 us; the launch traced here: 210 us
  Pallas kernels  91.9 us (44%)
  starting transfers between devices  55 us (26%)
  waiting for transfers between devices  27.5 us (13%)
  between operations  14.7 us (7%)
  other arithmetic  13.3 us (6%)
  local copies, waits for them, and re-layouts  7.12 us (3%)
    pallas_call x4, Pallas kernels, attention_backward(): pl.pallas_call(functools.partial(backward_kernel, slot, quarter // HEAD_S...  28.5 us
    ppermute x3, starting transfers between devices, paired(): return lax.ppermute(x, 'row', [(0, 1), (1, 0), (2, 3), (3, 2)])  17.9 us
    pallas_call x2, Pallas kernels, partial_products(): pl.pallas_call(partial_kernel, grid_spec=spec, out_shape=[jax.ShapeDtypeS...  17.7 us
    ppermute x4, starting transfers between devices, inward(): return lax.ppermute(x, 'row', [(0, 1), (3, 2)])  13 us
    pallas_call x1, Pallas kernels, weight_gradients(): pl.pallas_call(weights_kernel, grid=(feats // block,), in_specs=[pl.Block...  12.7 us
    pallas_call x2, Pallas kernels, attended_transposed(): pl.pallas_call(functools.partial(forward_kernel, [len(part) for part in p...  12.3 us
    pallas_call x2, Pallas kernels, input_gradients(): pl.pallas_call(functools.partial(input_kernel, half), grid_spec=spec, out...  12 us
    convert_element_type x7, other arithmetic, plus(): return sum((term.astype(F32) for term in terms)).astype(BF)  10.8 us
  transfers between devices with their start and end apart: 33, of which 9 were waited for; matrix products, arithmetic and copies ran while one was open for 5% of the time, Pallas kernels for 44%

profile of v3, /device:TPU:0, one launch (start us, length us, event | category | flops | bytes accessed | tf_op | source)
XLA Modules:
  0.0 209.6 jit_solution(11818428228498033342)
XLA Ops:
  8.4 5.4 %collective-permute-start.1 = (bf16[192,2048]{1,0:T(8,128)(2,1)}, bf16[192,2048]{1,0:T(8,128)(2,1)S(1)}, u32[]{:S(2)}, u32[]{:S(2)}) collective-permute-start(bf16[192,2048]{1,0:T(8,128)(2,1)} %rest_0_.7), channel_id=1, source_target_pairs={{0,4},{4,0},{8,12},{12,8},{1,5},{5,1},{9,13},{13,9},{2,6},{6,2},{1... | collective-permute-start | bytes 2359304 | tf_op jit(solution)/shard_map/ppermute | solution.py:463
  13.9 1.5 collective-permute-start
  17.6 8.9 %gradient_partial.2 = (bf16[384,512]{1,0:T(8,128)(2,1)}, bf16[768,512]{1,0:T(8,128)(2,1)}, bf16[384,512]{1,0:T(8,128)(2,1)}) custom-call(s32[28]{0:T(128)} %compare_select_fusion.8.place_ref, bf16[192,2048]{1,0:T(8,128)(2,1)} %first_ref.1, bf16[192,2048]{1,0:T(8,128)(2,1)} %copy-done.31, bf16[2048,2048]{1,0:T(8,128)(2,1)} %weight_ref.3), custom_call_target="tpu_custom_call" | custom-call | flops 1048576 | bytes 65536 | tf_op jit(solution)/shard_map/gradient_partial/pallas_call | solution.py:240
  26.5 5.5 %collective-permute-done.1.refs_1_.rest_1_ = bf16[192,2048]{1,0:T(8,128)(2,1)S(1)} collective-permute-done((bf16[192,2048]{1,0:T(8,128)(2,1)}, bf16[192,2048]{1,0:T(8,128)(2,1)S(1)}, u32[]{:S(2)}, u32[]{:S(2)}) %collective-permute-start.1) | collective-permute-done | bytes 786464 | tf_op jit(solution)/shard_map/ppermute | solution.py:463
  33.6 3.2 %collective-permute-start.4 = (bf16[384,512]{1,0:T(8,128)(2,1)}, bf16[384,512]{1,0:T(8,128)(2,1)}, u32[]{:S(2)}, u32[]{:S(2)}) collective-permute-start(bf16[384,512]{1,0:T(8,128)(2,1)} %get-tuple-element.105), channel_id=1, source_target_pairs={{0,4},{12,8},{1,5},{13,9},{2,6},{14,10},{3,7},{15,11},{16,20},{28,... | collective-permute-start | bytes 1179656 | tf_op jit(solution)/shard_map/ppermute | solution.py:451
  36.8 1.6 collective-permute-start.8
  39.7 5.6 %collective-permute-start.10 = (bf16[768,512]{1,0:T(8,128)(2,1)}, bf16[768,512]{1,0:T(8,128)(2,1)}, u32[]{:S(2)}, u32[]{:S(2)}) collective-permute-start(bf16[768,512]{1,0:T(8,128)(2,1)} %get-tuple-element.111), channel_id=1, source_target_pairs={{0,4},{12,8},{1,5},{13,9},{2,6},{14,10},{3,7},{15,11},{16,20},{28,... | collective-permute-start | bytes 2359304 | tf_op jit(solution)/shard_map/ppermute | solution.py:451
  45.2 8.9 %gradient_partial.3 = (bf16[384,512]{1,0:T(8,128)(2,1)}, bf16[768,512]{1,0:T(8,128)(2,1)}, bf16[384,512]{1,0:T(8,128)(2,1)}) custom-call(s32[28]{0:T(128)} %compare_select_fusion.8.place_ref, bf16[192,2048]{1,0:T(8,128)(2,1)} %copy-done.30, bf16[192,2048]{1,0:T(8,128)(2,1)} %collective-permute-done.5.second_ref, bf16[2048,2048]{1,0:T(8,128)(2,1)} %weight_ref.3), custom_call_target="tpu_custom_call" | custom-call | flops 1048576 | bytes 65536 | tf_op jit(solution)/shard_map/gradient_partial/pallas_call | solution.py:240
  54.1 1.9 add_convert_fusion.8
  56.8 2.8 %collective-permute-start.9 = (bf16[384,512]{1,0:T(8,128)(2,1)}, bf16[384,512]{1,0:T(8,128)(2,1)}, u32[]{:S(2)}, u32[]{:S(2)}) collective-permute-start(bf16[384,512]{1,0:T(8,128)(2,1)} %get-tuple-element.126), channel_id=1, source_target_pairs={{0,4},{12,8},{1,5},{13,9},{2,6},{14,10},{3,7},{15,11},{16,20},{28,... | collective-permute-start | bytes 1179656 | tf_op jit(solution)/shard_map/ppermute | solution.py:451
  61.1 1.5 collective-permute-done.10
  66.1 5.0 %collective-permute-done.9 = bf16[384,512]{1,0:T(8,128)(2,1)} collective-permute-done((bf16[384,512]{1,0:T(8,128)(2,1)}, bf16[384,512]{1,0:T(8,128)(2,1)}, u32[]{:S(2)}, u32[]{:S(2)}) %collective-permute-start.9) | collective-permute-done | bytes 393248 | tf_op jit(solution)/shard_map/ppermute | solution.py:451
  77.6 7.3 %attention_forward.2.refs_8_ = bf16[2048,768]{1,0:T(8,128)(2,1)S(1)} custom-call(s32[28]{0:T(128)S(1)} %copy-done.29, bf16[192,2048]{1,0:T(8,128)(2,1)S(1)} %copy-done.3, bf16[192,2048]{1,0:T(8,128)(2,1)S(1)} %copy-done.10, bf16[192,2048]{1,0:T(8,128)(2,1)S(1)} %copy-done.13, bf16[192,2048]{1,0:T(8,128)(2,1)S(1)} %copy-done.7, ...), custom_call_target="tpu_custom_call" | custom-call | flops 1048576 | bytes 65536 | tf_op jit(solution)/shard_map/attention_forward/pallas_call | solution.py:108
  87.8 6.3 %collective-permute-start.14 = (bf16[384,512]{1,0:T(8,128)(2,1)S(1)}, bf16[384,512]{1,0:T(8,128)(2,1)}, u32[]{:S(2)}, u32[]{:S(2)}) collective-permute-start(bf16[384,512]{1,0:T(8,128)(2,1)S(1)} %add_convert_fusion.5.rest_6_), channel_id=1, source_target_pairs={{0,4},{4,0},{8,12},{12,8},{1,5},{5,1},{9,13},{13,9},{2,6},{6,2},{1... | collective-permute-start | bytes 1179656 | tf_op jit(solution)/shard_map/ppermute | solution.py:463
  97.9 1.6 collective-permute-done.11.refs_4_.rest_4_
  99.5 5.0 %attention_forward.3.attended_ref = bf16[2048,768]{1,0:T(8,128)(2,1)S(1)} custom-call(s32[28]{0:T(128)S(1)} %copy-done.29, bf16[192,2048]{1,0:T(8,128)(2,1)S(1)} %copy-done.4, bf16[192,2048]{1,0:T(8,128)(2,1)S(1)} %copy-done.10, bf16[192,2048]{1,0:T(8,128)(2,1)S(1)} %copy-done.14, bf16[192,2048]{1,0:T(8,128)(2,1)S(1)} %copy-done.7, ...), custom_call_target="tpu_custom_call", output_to_operand_aliasing={{}: (9, {})} | custom-call | flops 1048576 | bytes 65536 | tf_op jit(solution)/shard_map/attention_forward/pallas_call | solution.py:108
  104.6 3.5 %collective-permute-done.14.rest_6_ = bf16[384,512]{1,0:T(8,128)(2,1)} collective-permute-done((bf16[384,512]{1,0:T(8,128)(2,1)S(1)}, bf16[384,512]{1,0:T(8,128)(2,1)}, u32[]{:S(2)}, u32[]{:S(2)}) %collective-permute-start.14) | collective-permute-done | bytes 393248 | tf_op jit(solution)/shard_map/ppermute | solution.py:463
  110.8 1.9 copy-done.24
  112.7 8.6 %output_gradient.1 = bf16[2048,2048]{1,0:T(8,128)(2,1)} custom-call(bf16[2048,768]{1,0:T(8,128)(2,1)S(1)} %attention_forward.3.attended_ref, bf16[768,2048]{1,0:T(8,128)(2,1)S(1)} %copy-done.24), custom_call_target="tpu_custom_call" | custom-call | flops 1048576 | bytes 65536 | tf_op jit(solution)/shard_map/output_gradient/pallas_call | solution.py:257
  123.4 6.2 %collective-permute-start.23 = (bf16[384,512]{1,0:T(8,128)(2,1)S(1)}, bf16[384,512]{1,0:T(8,128)(2,1)S(1)}, u32[]{:S(2)}, u32[]{:S(2)}) collective-permute-start(bf16[384,512]{1,0:T(8,128)(2,1)S(1)} %add_convert_fusion.1.rest_7_), channel_id=1, source_target_pairs={{0,4},{4,0},{8,12},{12,8},{1,5},{5,1},{9,13},{13,9},{2,6},{6,2},{1... | collective-permute-start | bytes 1179656 | tf_op jit(solution)/shard_map/ppermute | solution.py:463
  129.6 6.7 %attention_backward.4 = (bf16[768,2048]{1,0:T(8,128)(2,1)S(1)}, f32[768,256]{1,0:T(8,128)S(1)}, f32[768,256]{1,0:T(8,128)S(1)}) custom-call(s32[28]{0:T(128)S(1)} %copy-done.29, bf16[768,256]{1,0:T(8,128)(2,1)S(1)} %copy-done.18, bf16[768,256]{1,0:T(8,128)(2,1)S(1)} %copy-done.21, bf16[192,2048]{1,0:T(8,128)(2,1)S(1)} %copy-done.5, ...), custom_call_target="tpu_custom_call" | custom-call | flops 1048576 | bytes 65536 | tf_op jit(solution)/shard_map/attention_backward/pallas_call | solution.py:191
  139.8 7.0 %attention_backward.5 = (bf16[768,2048]{1,0:T(8,128)(2,1)S(1)}, f32[768,256]{1,0:T(8,128)S(1)}, f32[768,256]{1,0:T(8,128)S(1)}) custom-call(s32[28]{0:T(128)S(1)} %copy-done.29, bf16[768,256]{1,0:T(8,128)(2,1)S(1)} %copy-done.18, bf16[768,256]{1,0:T(8,128)(2,1)S(1)} %copy-done.21, ...), custom_call_target="tpu_custom_call", output_to_operand_aliasing={{0}: (11, {}), {1}: (12, {}), {2}: (13, {})} | custom-call | flops 1048576 | bytes 65536 | tf_op jit(solution)/shard_map/attention_backward/pallas_call | solution.py:191
  146.8 4.4 %collective-permute-done.26.rest_8_ = bf16[384,512]{1,0:T(8,128)(2,1)S(1)} collective-permute-done((bf16[384,512]{1,0:T(8,128)(2,1)S(1)}, bf16[384,512]{1,0:T(8,128)(2,1)S(1)}, u32[]{:S(2)}, u32[]{:S(2)}) %collective-permute-start.26) | collective-permute-done | bytes 393248 | tf_op jit(solution)/shard_map/ppermute | solution.py:459
  152.5 7.5 %attention_backward.6 = (bf16[768,2048]{1,0:T(8,128)(2,1)S(1)}, f32[768,256]{1,0:T(8,128)S(1)}, f32[768,256]{1,0:T(8,128)S(1)}) custom-call(s32[28]{0:T(128)S(1)} %copy-done.29, bf16[768,256]{1,0:T(8,128)(2,1)S(1)} %copy-done.18, bf16[768,256]{1,0:T(8,128)(2,1)S(1)} %copy-done.21, ...), custom_call_target="tpu_custom_call", output_to_operand_aliasing={{0}: (13, {}), {1}: (14, {}), {2}: (15, {})} | custom-call | flops 1048576 | bytes 65536 | tf_op jit(solution)/shard_map/attention_backward/pallas_call | solution.py:191
  160.0 2.2 %collective-permute-done.27.rest_8_ = bf16[384,512]{1,0:T(8,128)(2,1)S(1)} collective-permute-done((bf16[384,512]{1,0:T(8,128)(2,1)S(1)}, bf16[384,512]{1,0:T(8,128)(2,1)S(1)}, u32[]{:S(2)}, u32[]{:S(2)}) %collective-permute-start.27) | collective-permute-done | bytes 393248 | tf_op jit(solution)/shard_map/ppermute | solution.py:459
  162.2 7.4 %attention_backward.7 = (bf16[768,2048]{1,0:T(8,128)(2,1)S(1)}, f32[768,256]{1,0:T(8,128)S(1)}, f32[768,256]{1,0:T(8,128)S(1)}) custom-call(s32[28]{0:T(128)S(1)} %copy-done.29, bf16[768,256]{1,0:T(8,128)(2,1)S(1)} %copy-done.18, bf16[768,256]{1,0:T(8,128)(2,1)S(1)} %copy-done.21, ...), custom_call_target="tpu_custom_call", output_to_operand_aliasing={{0}: (13, {}), {1}: (14, {}), {2}: (15, {})} | custom-call | flops 1048576 | bytes 65536 | tf_op jit(solution)/shard_map/attention_backward/pallas_call | solution.py:191
  169.7 5.7 %input_gradients.2 = (bf16[192,2048]{1,0:T(8,128)(2,1)S(1)}, bf16[192,2048]{1,0:T(8,128)(2,1)S(1)}) custom-call(s32[28]{0:T(128)S(1)} %copy-done.29, bf16[768,2048]{1,0:T(8,128)(2,1)S(1)} %get-tuple-element.174.dq_ref, f32[768,256]{1,0:T(8,128)S(1)} %get-tuple-element.175.dk_ref, f32[768,256]{1,0:T(8,128)S(1)} %get-tuple-element.176.dv_ref, ...), custom_call_target="tpu_custom_call" | custom-call | flops 1048576 | bytes 65536 | tf_op jit(solution)/shard_map/input_gradients/pallas_call | solution.py:311
  175.4 2.3 %collective-permute-done.28 = bf16[192,2048]{1,0:T(8,128)(2,1)S(1)} collective-permute-done((bf16[192,2048]{1,0:T(8,128)(2,1)S(1)}, bf16[192,2048]{1,0:T(8,128)(2,1)S(1)}, u32[]{:S(2)}, u32[]{:S(2)}) %collective-permute-start.28) | collective-permute-done | bytes 786464 | tf_op jit(solution)/shard_map/ppermute | solution.py:447
  178.9 1.5 collective-permute-start.30
  180.4 6.3 %input_gradients.3 = (bf16[192,2048]{1,0:T(8,128)(2,1)}, bf16[192,2048]{1,0:T(8,128)(2,1)S(1)}) custom-call(s32[28]{0:T(128)S(1)} %copy-done.29, bf16[768,2048]{1,0:T(8,128)(2,1)S(1)} %get-tuple-element.174.dq_ref, f32[768,256]{1,0:T(8,128)S(1)} %get-tuple-element.175.dk_ref, f32[768,256]{1,0:T(8,128)S(1)} %get-tuple-element.176.dv_ref, ...), custom_call_target="tpu_custom_call" | custom-call | flops 1048576 | bytes 65536 | tf_op jit(solution)/shard_map/input_gradients/pallas_call | solution.py:311
  187.6 12.7 %weight_gradients.1 = (bf16[2048,2048]{1,0:T(8,128)(2,1)}, bf16[2048,256]{1,0:T(8,128)(2,1)}, bf16[2048,256]{1,0:T(8,128)(2,1)}) custom-call(bf16[768,2048]{1,0:T(8,128)(2,1)} %all-gather.3.cloned.1.call-done.n_ref, bf16[768,2048]{1,0:T(8,128)(2,1)} %copy-done, f32[768,256]{1,0:T(8,128)} %copy-done.1, f32[768,256]{1,0:T(8,128)} %copy-done.2), custom_call_target="tpu_custom_call" | custom-call | flops 1048576 | bytes 65536 | tf_op jit(solution)/shard_map/weight_gradients/pallas_call | solution.py:279
  200.3 2.4 %add_convert_fusion = bf16[192,2048]{1,0:T(8,128)(2,1)} fusion(bf16[192,2048]{1,0:T(8,128)(2,1)} %collective-permute-done.30, bf16[192,2048]{1,0:T(8,128)(2,1)S(1)} %collective-permute-done.29, bf16[192,2048]{1,0:T(8,128)(2,1)S(1)} %copy-done.28), kind=kLoop, calls=%fused_computation | loop fusion | flops 2359296 | bytes 3145728 | tf_op jit(solution)/shard_map/convert_element_type | solution.py:471
  (142 shorter events, 36.8 us)
Async XLA Ops:
  7.2 103.6 %all-gather.5.cloned.1.call-start = ((), (), s32[]{:S(2)}) async-start(), calls=%async_computation.1 | async-start | bytes 3932160 | tf_op jit(solution)/shard_map/all_gather | solution.py:528
  7.2 9.5 %collective-permute-start.3 = (bf16[192,2048]{1,0:T(8,128)(2,1)}, bf16[192,2048]{1,0:T(8,128)(2,1)S(1)}, u32[]{:S(2)}, u32[]{:S(2)}) collective-permute-start(bf16[192,2048]{1,0:T(8,128)(2,1)} %first_ref.1), channel_id=1, source_target_pairs={{0,1},{1,0},{2,3},{3,2},{4,5},{5,4},{6,7},{7,6},{8,9},{9,8},{10,11... | collective-permute-start | bytes 2359304 | tf_op jit(solution)/shard_map/ppermute | solution.py:447
  7.7 18.7 %collective-permute-start.2 = (bf16[192,2048]{1,0:T(8,128)(2,1)}, bf16[192,2048]{1,0:T(8,128)(2,1)S(1)}, u32[]{:S(2)}, u32[]{:S(2)}) collective-permute-start(bf16[192,2048]{1,0:T(8,128)(2,1)} %rest_0_.7), channel_id=1, source_target_pairs={{4,8},{8,4},{5,9},{9,5},{6,10},{10,6},{7,11},{11,7},{20,24},{24,20... | collective-permute-start | bytes 2359304 | tf_op jit(solution)/shard_map/ppermute | solution.py:455
  8.4 23.6 %collective-permute-start.1 = (bf16[192,2048]{1,0:T(8,128)(2,1)}, bf16[192,2048]{1,0:T(8,128)(2,1)S(1)}, u32[]{:S(2)}, u32[]{:S(2)}) collective-permute-start(bf16[192,2048]{1,0:T(8,128)(2,1)} %rest_0_.7), channel_id=1, source_target_pairs={{0,4},{4,0},{8,12},{12,8},{1,5},{5,1},{9,13},{13,9},{2,6},{6,2},{1... | collective-permute-start | bytes 2359304 | tf_op jit(solution)/shard_map/ppermute | solution.py:463
  13.9 19.6 %collective-permute-start = (bf16[192,2048]{1,0:T(8,128)(2,1)}, bf16[192,2048]{1,0:T(8,128)(2,1)S(1)}, u32[]{:S(2)}, u32[]{:S(2)}) collective-permute-start(bf16[192,2048]{1,0:T(8,128)(2,1)} %first_ref.1), channel_id=1, source_target_pairs={{0,2},{2,0},{1,3},{3,1},{4,6},{6,4},{5,7},{7,5},{8,10},{10,8},{9,1... | collective-permute-start | bytes 2359304 | tf_op jit(solution)/shard_map/ppermute | solution.py:447
  33.5 154.1 %all-gather.3.cloned.1.call-start = ((), (), s32[]{:S(2)}) async-start(), calls=%async_computation | async-start | bytes 3932160 | tf_op jit(solution)/shard_map/all_gather | solution.py:529
  33.5 11.7 %collective-permute-start.5 = (bf16[192,2048]{1,0:T(8,128)(2,1)S(1)}, bf16[192,2048]{1,0:T(8,128)(2,1)}, u32[]{:S(2)}, u32[]{:S(2)}) collective-permute-start(bf16[192,2048]{1,0:T(8,128)(2,1)S(1)} %collective-permute-done.first_ref), channel_id=1, source_target_pairs={{0,1},{1,0},{2,3},{3,2},{4,5},{5,4},{6,7},{7,6},{8,9},{9,8},{10,11... | collective-permute-start | bytes 2359304 | tf_op jit(solution)/shard_map/ppermute | solution.py:447
  33.6 20.5 %collective-permute-start.4 = (bf16[384,512]{1,0:T(8,128)(2,1)}, bf16[384,512]{1,0:T(8,128)(2,1)}, u32[]{:S(2)}, u32[]{:S(2)}) collective-permute-start(bf16[384,512]{1,0:T(8,128)(2,1)} %get-tuple-element.105), channel_id=1, source_target_pairs={{0,4},{12,8},{1,5},{13,9},{2,6},{14,10},{3,7},{15,11},{16,20},{28,... | collective-permute-start | bytes 1179656 | tf_op jit(solution)/shard_map/ppermute | solution.py:451
  36.8 22.8 %collective-permute-start.8 = (bf16[192,2048]{1,0:T(8,128)(2,1)S(1)}, bf16[192,2048]{1,0:T(8,128)(2,1)}, u32[]{:S(2)}, u32[]{:S(2)}) collective-permute-start(bf16[192,2048]{1,0:T(8,128)(2,1)S(1)} %collective-permute-done.1.refs_1_.rest_1_), channel_id=1, source_target_pairs={{4,8},{8,4},{5,9},{9,5},{6,10},{10,6},{7,11},{11,7},{20,24},{24,20... | collective-permute-start | bytes 2359304 | tf_op jit(solution)/shard_map/ppermute | solution.py:455
  38.4 22.7 %collective-permute-start.7 = (bf16[192,2048]{1,0:T(8,128)(2,1)S(1)}, bf16[192,2048]{1,0:T(8,128)(2,1)S(1)}, u32[]{:S(2)}, u32[]{:S(2)}) collective-permute-start(bf16[192,2048]{1,0:T(8,128)(2,1)S(1)} %collective-permute-done.2.refs_3_.rest_3_), channel_id=1, source_target_pairs={{4,0},{8,12},{5,1},{9,13},{6,2},{10,14},{7,3},{11,15},{20,16},{24,... | collective-permute-start | bytes 2359304 | tf_op jit(solution)/shard_map/ppermute | solution.py:459
  39.7 23.0 %collective-permute-start.10 = (bf16[768,512]{1,0:T(8,128)(2,1)}, bf16[768,512]{1,0:T(8,128)(2,1)}, u32[]{:S(2)}, u32[]{:S(2)}) collective-permute-start(bf16[768,512]{1,0:T(8,128)(2,1)} %get-tuple-element.111), channel_id=1, source_target_pairs={{0,4},{12,8},{1,5},{13,9},{2,6},{14,10},{3,7},{15,11},{16,20},{28,... | collective-permute-start | bytes 2359304 | tf_op jit(solution)/shard_map/ppermute | solution.py:451
  56.1 5.0 %collective-permute-start.6 = (bf16[384,512]{1,0:T(8,128)(2,1)}, bf16[384,512]{1,0:T(8,128)(2,1)S(1)}, u32[]{:S(2)}, u32[]{:S(2)}) collective-permute-start(bf16[384,512]{1,0:T(8,128)(2,1)} %add_convert_fusion.8), channel_id=1, source_target_pairs={{4,8},{8,4},{5,9},{9,5},{6,10},{10,6},{7,11},{11,7},{20,24},{24,20... | collective-permute-start | bytes 1179656 | tf_op jit(solution)/shard_map/ppermute | solution.py:455
  56.8 14.3 %collective-permute-start.9 = (bf16[384,512]{1,0:T(8,128)(2,1)}, bf16[384,512]{1,0:T(8,128)(2,1)}, u32[]{:S(2)}, u32[]{:S(2)}) collective-permute-start(bf16[384,512]{1,0:T(8,128)(2,1)} %get-tuple-element.126), channel_id=1, source_target_pairs={{0,4},{12,8},{1,5},{13,9},{2,6},{14,10},{3,7},{15,11},{16,20},{28,... | collective-permute-start | bytes 1179656 | tf_op jit(solution)/shard_map/ppermute | solution.py:451
  59.6 34.4 %collective-permute-start.19 = (bf16[768,512]{1,0:T(8,128)(2,1)}, bf16[768,512]{1,0:T(8,128)(2,1)S(1)}, u32[]{:S(2)}, u32[]{:S(2)}) collective-permute-start(bf16[768,512]{1,0:T(8,128)(2,1)} %get-tuple-element.129), channel_id=1, source_target_pairs={{0,4},{12,8},{1,5},{13,9},{2,6},{14,10},{3,7},{15,11},{16,20},{28,... | collective-permute-start | bytes 2359304 | tf_op jit(solution)/shard_map/ppermute | solution.py:451
  64.1 20.9 %collective-permute-start.13 = (bf16[384,512]{1,0:T(8,128)(2,1)S(1)}, bf16[384,512]{1,0:T(8,128)(2,1)S(1)}, u32[]{:S(2)}, u32[]{:S(2)}) collective-permute-start(bf16[384,512]{1,0:T(8,128)(2,1)S(1)} %get-tuple-element.193), channel_id=1, source_target_pairs={{4,8},{8,4},{5,9},{9,5},{6,10},{10,6},{7,11},{11,7},{20,24},{24,20... | collective-permute-start | bytes 1179656 | tf_op jit(solution)/shard_map/ppermute | solution.py:455
  64.8 20.2 %collective-permute-start.12 = (bf16[384,512]{1,0:T(8,128)(2,1)S(1)}, bf16[384,512]{1,0:T(8,128)(2,1)S(1)}, u32[]{:S(2)}, u32[]{:S(2)}) collective-permute-start(bf16[384,512]{1,0:T(8,128)(2,1)S(1)} %get-tuple-element.194), channel_id=1, source_target_pairs={{4,0},{8,12},{5,1},{9,13},{6,2},{10,14},{7,3},{11,15},{20,16},{24,... | collective-permute-start | bytes 1179656 | tf_op jit(solution)/shard_map/ppermute | solution.py:459
  72.3 21.8 %collective-permute-start.18 = (bf16[384,512]{1,0:T(8,128)(2,1)S(1)}, bf16[384,512]{1,0:T(8,128)(2,1)S(1)}, u32[]{:S(2)}, u32[]{:S(2)}) collective-permute-start(bf16[384,512]{1,0:T(8,128)(2,1)S(1)} %add_convert_fusion.4), channel_id=1, source_target_pairs={{4,8},{8,4},{5,9},{9,5},{6,10},{10,6},{7,11},{11,7},{20,24},{24,20... | collective-permute-start | bytes 1179656 | tf_op jit(solution)/shard_map/ppermute | solution.py:455
  73.0 26.5 %collective-permute-start.11 = (bf16[192,2048]{1,0:T(8,128)(2,1)}, bf16[192,2048]{1,0:T(8,128)(2,1)S(1)}, u32[]{:S(2)}, u32[]{:S(2)}) collective-permute-start(bf16[192,2048]{1,0:T(8,128)(2,1)} %collective-permute-done.8.refs_5_.rest_5_), channel_id=1, source_target_pairs={{4,0},{8,12},{5,1},{9,13},{6,2},{10,14},{7,3},{11,15},{20,16},{24,... | collective-permute-start | bytes 2359304 | tf_op jit(solution)/shard_map/ppermute | solution.py:459
  86.3 18.2 %collective-permute-start.15 = (bf16[384,512]{1,0:T(8,128)(2,1)S(1)}, bf16[384,512]{1,0:T(8,128)(2,1)}, u32[]{:S(2)}, u32[]{:S(2)}) collective-permute-start(bf16[384,512]{1,0:T(8,128)(2,1)S(1)} %add_convert_fusion.5.rest_6_), channel_id=1, source_target_pairs={{4,8},{8,4},{5,9},{9,5},{6,10},{10,6},{7,11},{11,7},{20,24},{24,20... | collective-permute-start | bytes 1179656 | tf_op jit(solution)/shard_map/ppermute | solution.py:455
  87.8 20.3 %collective-permute-start.14 = (bf16[384,512]{1,0:T(8,128)(2,1)S(1)}, bf16[384,512]{1,0:T(8,128)(2,1)}, u32[]{:S(2)}, u32[]{:S(2)}) collective-permute-start(bf16[384,512]{1,0:T(8,128)(2,1)S(1)} %add_convert_fusion.5.rest_6_), channel_id=1, source_target_pairs={{0,4},{4,0},{8,12},{12,8},{1,5},{5,1},{9,13},{13,9},{2,6},{6,2},{1... | collective-permute-start | bytes 1179656 | tf_op jit(solution)/shard_map/ppermute | solution.py:463
  95.2 26.1 %collective-permute-start.21 = (bf16[384,512]{1,0:T(8,128)(2,1)}, bf16[384,512]{1,0:T(8,128)(2,1)}, u32[]{:S(2)}, u32[]{:S(2)}) collective-permute-start(bf16[384,512]{1,0:T(8,128)(2,1)} %get-tuple-element.191), channel_id=1, source_target_pairs={{4,8},{8,4},{5,9},{9,5},{6,10},{10,6},{7,11},{11,7},{20,24},{24,20... | collective-permute-start | bytes 1179656 | tf_op jit(solution)/shard_map/ppermute | solution.py:455
  96.6 24.7 %collective-permute-start.20 = (bf16[384,512]{1,0:T(8,128)(2,1)}, bf16[384,512]{1,0:T(8,128)(2,1)}, u32[]{:S(2)}, u32[]{:S(2)}) collective-permute-start(bf16[384,512]{1,0:T(8,128)(2,1)} %get-tuple-element.192), channel_id=1, source_target_pairs={{4,0},{8,12},{5,1},{9,13},{6,2},{10,14},{7,3},{11,15},{20,16},{24,... | collective-permute-start | bytes 1179656 | tf_op jit(solution)/shard_map/ppermute | solution.py:459
  108.0 28.3 %collective-permute-start.16 = (bf16[384,512]{1,0:T(8,128)(2,1)}, bf16[384,512]{1,0:T(8,128)(2,1)}, u32[]{:S(2)}, u32[]{:S(2)}) collective-permute-start(bf16[384,512]{1,0:T(8,128)(2,1)} %collective-permute-done.14.rest_6_), channel_id=1, source_target_pairs={{4,8},{8,4},{5,9},{9,5},{6,10},{10,6},{7,11},{11,7},{20,24},{24,20... | collective-permute-start | bytes 1179656 | tf_op jit(solution)/shard_map/ppermute | solution.py:455
  109.4 26.9 %collective-permute-start.17 = (bf16[384,512]{1,0:T(8,128)(2,1)}, bf16[384,512]{1,0:T(8,128)(2,1)}, u32[]{:S(2)}, u32[]{:S(2)}) collective-permute-start(bf16[384,512]{1,0:T(8,128)(2,1)} %collective-permute-done.15.rest_7_), channel_id=1, source_target_pairs={{4,0},{8,12},{5,1},{9,13},{6,2},{10,14},{7,3},{11,15},{20,16},{24,... | collective-permute-start | bytes 1179656 | tf_op jit(solution)/shard_map/ppermute | solution.py:459
  122.7 13.7 %collective-permute-start.24 = (bf16[384,512]{1,0:T(8,128)(2,1)S(1)}, bf16[384,512]{1,0:T(8,128)(2,1)S(1)}, u32[]{:S(2)}, u32[]{:S(2)}) collective-permute-start(bf16[384,512]{1,0:T(8,128)(2,1)S(1)} %add_convert_fusion.1.rest_7_), channel_id=1, source_target_pairs={{4,8},{8,4},{5,9},{9,5},{6,10},{10,6},{7,11},{11,7},{20,24},{24,20... | collective-permute-start | bytes 1179656 | tf_op jit(solution)/shard_map/ppermute | solution.py:455
  123.4 13.0 %collective-permute-start.23 = (bf16[384,512]{1,0:T(8,128)(2,1)S(1)}, bf16[384,512]{1,0:T(8,128)(2,1)S(1)}, u32[]{:S(2)}, u32[]{:S(2)}) collective-permute-start(bf16[384,512]{1,0:T(8,128)(2,1)S(1)} %add_convert_fusion.1.rest_7_), channel_id=1, source_target_pairs={{0,4},{4,0},{8,12},{12,8},{1,5},{5,1},{9,13},{13,9},{2,6},{6,2},{1... | collective-permute-start | bytes 1179656 | tf_op jit(solution)/shard_map/ppermute | solution.py:463
  136.3 10.5 %collective-permute-start.25 = (bf16[384,512]{1,0:T(8,128)(2,1)S(1)}, bf16[384,512]{1,0:T(8,128)(2,1)S(1)}, u32[]{:S(2)}, u32[]{:S(2)}) collective-permute-start(bf16[384,512]{1,0:T(8,128)(2,1)S(1)} %collective-permute-done.23.rest_7_), channel_id=1, source_target_pairs={{4,8},{8,4},{5,9},{9,5},{6,10},{10,6},{7,11},{11,7},{20,24},{24,20... | collective-permute-start | bytes 1179656 | tf_op jit(solution)/shard_map/ppermute | solution.py:455
  137.0 14.2 %collective-permute-start.26 = (bf16[384,512]{1,0:T(8,128)(2,1)S(1)}, bf16[384,512]{1,0:T(8,128)(2,1)S(1)}, u32[]{:S(2)}, u32[]{:S(2)}) collective-permute-start(bf16[384,512]{1,0:T(8,128)(2,1)S(1)} %collective-permute-done.24.rest_9_), channel_id=1, source_target_pairs={{4,0},{8,12},{5,1},{9,13},{6,2},{10,14},{7,3},{11,15},{20,16},{24,... | collective-permute-start | bytes 1179656 | tf_op jit(solution)/shard_map/ppermute | solution.py:459
  138.5 21.5 %collective-permute-start.22 = (bf16[384,512]{1,0:T(8,128)(2,1)}, bf16[384,512]{1,0:T(8,128)(2,1)S(1)}, u32[]{:S(2)}, u32[]{:S(2)}) collective-permute-start(bf16[384,512]{1,0:T(8,128)(2,1)} %collective-permute-done.16.rest_7_), channel_id=1, source_target_pairs={{4,0},{8,12},{5,1},{9,13},{6,2},{10,14},{7,3},{11,15},{20,16},{24,... | collective-permute-start | bytes 1179656 | tf_op jit(solution)/shard_map/ppermute | solution.py:459
  151.2 11.0 %collective-permute-start.27 = (bf16[384,512]{1,0:T(8,128)(2,1)S(1)}, bf16[384,512]{1,0:T(8,128)(2,1)S(1)}, u32[]{:S(2)}, u32[]{:S(2)}) collective-permute-start(bf16[384,512]{1,0:T(8,128)(2,1)S(1)} %collective-permute-done.25.rest_9_), channel_id=1, source_target_pairs={{4,0},{8,12},{5,1},{9,13},{6,2},{10,14},{7,3},{11,15},{20,16},{24,... | collective-permute-start | bytes 1179656 | tf_op jit(solution)/shard_map/ppermute | solution.py:459
  178.9 21.5 %collective-permute-start.30 = (bf16[192,2048]{1,0:T(8,128)(2,1)}, bf16[192,2048]{1,0:T(8,128)(2,1)}, u32[]{:S(2)}, u32[]{:S(2)}) collective-permute-start(bf16[192,2048]{1,0:T(8,128)(2,1)} %add.61), channel_id=1, source_target_pairs={{0,2},{2,0},{1,3},{3,1},{4,6},{6,4},{5,7},{7,5},{8,10},{10,8},{9,1... | collective-permute-start | bytes 2359304 | tf_op jit(solution)/shard_map/ppermute | solution.py:447
  187.6 12.7 %collective-permute-start.29 = (bf16[192,2048]{1,0:T(8,128)(2,1)}, bf16[192,2048]{1,0:T(8,128)(2,1)S(1)}, u32[]{:S(2)}, u32[]{:S(2)}) collective-permute-start(bf16[192,2048]{1,0:T(8,128)(2,1)} %get-tuple-element.182), channel_id=1, source_target_pairs={{0,1},{1,0},{2,3},{3,2},{4,5},{5,4},{6,7},{7,6},{8,9},{9,8},{10,11... | collective-permute-start | bytes 2359304 | tf_op jit(solution)/shard_map/ppermute | solution.py:447
  (42 other events, 517.7 us)
Sparse Core Ops, SparseCore 0:
  33.6 27.5 all-gather.4
  62.7 28.5 all-gather.2
